TPU v7x, 32 devices: a whole 2x2x4 slice. The times are simulated.
32 devices in a mesh: rows: 4 (over y, x), bytes: 8 (over z, core).
Axes of the slice: x: 2, y: 2, z: 4, core: 2. Of those that a mesh axis runs over, the one named last changes fastest.
Arguments:
- tokens: bfloat16 [8, 1024, 1024], P('rows', 'bytes'), may hold values from -6 to 6
- boundaries: int32 [8, 16], P('rows'), may hold values from 1 to 1024, as said below
- norm_gain: float32 [2, 1024], replicated, may hold values from 0.25 to 1.75
- in_weight: bfloat16 [2, 4096, 1024], P(None, ('rows', 'bytes')), may hold values from -0.1875 to 0.1875
- out_weight: bfloat16 [2, 2048, 1024], P(None, ('rows', 'bytes')), may hold values from -0.375 to 0.375
- conv_weight: float32 [2, 4, 2048], P(None, None, 'bytes'), may hold values from -3 to 3
- conv_bias: float32 [2, 2048], P(None, 'bytes'), may hold values from -0.5 to 0.5
- xproj_weight: bfloat16 [2, 2048, 96], P(None, 'bytes'), may hold values from -0.25 to 0.25
- dtproj_weight: bfloat16 [2, 64, 2048], P(None, None, 'bytes'), may hold values from -0.75 to 0.75
- dt_bias: float32 [2, 2048], P(None, 'bytes'), may hold values from -5 to -3
- decay_log: float32 [2, 16, 2048], P(None, None, 'bytes'), may hold values from -11 to 0.5
- skip_gain: float32 [2, 2048], P(None, 'bytes'), may hold values from 0.5 to 1.5
- cotangent: bfloat16 [8, 1024, 1024], P('rows', 'bytes'), may hold values from -6 to 6
Outputs:
- activations: float32 [8, 1024, 1024], P('rows', 'bytes')
- grad_tokens: float32 [8, 1024, 1024], P('rows', 'bytes')
- grad_norm_gain: float32 [2, 1024], replicated
- grad_in_weight: float32 [2, 4096, 1024], P(None, ('rows', 'bytes'))
- grad_out_weight: float32 [2, 2048, 1024], P(None, ('rows', 'bytes'))
- grad_conv_weight: float32 [2, 4, 2048], P(None, None, 'bytes')
- grad_conv_bias: float32 [2, 2048], P(None, 'bytes')
- grad_xproj_weight: float32 [2, 2048, 96], P(None, 'bytes')
- grad_dtproj_weight: float32 [2, 64, 2048], P(None, None, 'bytes')
- grad_dt_bias: float32 [2, 2048], P(None, 'bytes')
- grad_decay_log: float32 [2, 16, 2048], P(None, None, 'bytes')
- grad_skip_gain: float32 [2, 2048], P(None, 'bytes')
Inputs may be any that keep to these rules, and one draw needn't show every extreme that they name: `boundaries`: each row lists the first positions of its later segments in rising order, repeats allowed, then 1024 in unused slots; in every aligned group of 2 rows exactly one row holds 1024 only.
All inputs are finite; a program needn't handle non-finite values.
Results may differ from a plain program's by a relative error of at most 0.02385.
Values may be sent and summed in bfloat16 or wider, within the bound.
A program may use at most 768 MiB of HBM per device.

v0:
```python
import functools

import jax
import jax.numpy as jnp
from jax import lax
from jax.experimental import pallas as pl
from jax.experimental.pallas import tpu as pltpu
from jax.sharding import PartitionSpec as P

norm_eps = 1e-05
f32 = jnp.float32
bf16 = jnp.bfloat16
STEPS = 8
CB = 256
KILL = 1e30
LOG2E = 1.4426950408889634
VMEM = 48 * 2**20

NT = (((1,), (1,)), ((), ()))


def dot(a, b):
    return jnp.dot(a, b, preferred_element_type=f32)


def dot_nt(a, b):
    return lax.dot_general(a, b, NT, preferred_element_type=f32)


def halves(v):
    high = v.astype(bf16)
    return high, (v - high.astype(f32)).astype(bf16)


def wide(v, width):
    return jnp.concatenate([v] * (width // v.shape[1]), axis=1)


def sigmoid(v):
    return 1.0 / (1.0 + jnp.exp(-v))


def conv_sum(x, halo, kernel, offset, masks, rows):
    length = x.shape[0] // rows
    taps = kernel.shape[0]
    outs = []
    for s in range(rows):
        ext = jnp.concatenate([halo[8 * s : 8 * s + 8], x[s * length : (s + 1) * length]], axis=0)
        total = offset + kernel[taps - 1 : taps] * ext[8:]
        for lag in range(1, taps):
            moved = pltpu.roll(ext, lag, 0)[8:]
            m = masks[lag - 1][s * length : (s + 1) * length]
            total = total + kernel[taps - 1 - lag : taps - lag] * moved * m
        outs.append(total)
    return jnp.concatenate(outs, axis=0)


def conv_kernel(rows, x_ref, halo_ref, kern_ref, off_ref, mask_ref, xp_ref, act_ref, proj_ref):
    @pl.when(pl.program_id(0) == 0)
    def _():
        proj_ref[...] = jnp.zeros_like(proj_ref)

    x = x_ref[...].astype(bf16).astype(f32)
    cb = x.shape[1]
    masks = [wide(mask_ref[i], cb) for i in range(mask_ref.shape[0])]
    pre = conv_sum(x, halo_ref[...].astype(f32), kern_ref[...], off_ref[...], masks, rows)
    act = pre * sigmoid(pre)
    act_ref[...] = act
    high, low = halves(act)
    weight = xp_ref[...]
    proj_ref[...] += dot_nt(high, weight) + dot_nt(low, weight)


def step_sizes(rank2_ref, dtw_ref, bias_ref):
    weight = dtw_ref[...]
    pre = dot(rank2_ref[...], jnp.concatenate([weight, weight], axis=0)) + bias_ref[...]
    return jnp.maximum(pre, 0.0) + jnp.log1p(jnp.exp(-jnp.abs(pre)))


def chunked(v):
    return v.reshape(v.shape[0] // STEPS, STEPS, v.shape[1])


def tokens_of(ref, rows, k):
    per = ref.shape[0] // rows
    return jnp.concatenate([ref[s * per + k] for s in range(rows)], axis=0)


def drive_of(bd_ref, u_ref, rows, k):
    high, low = halves(tokens_of(u_ref, rows, k))
    return dot(bd_ref[k], jnp.concatenate([high, low, high], axis=0))


def ends_kernel(rows, act_ref, rank2_ref, dtw_ref, bias_ref, kill_ref, rate_ref, bd_ref,
                delta_ref, end_ref, sum_ref, eff_s, u_s, drive_s):
    delta = step_sizes(rank2_ref, dtw_ref, bias_ref)
    cb = delta.shape[1]
    delta_ref[...] = delta
    eff = delta + wide(kill_ref[...], cb)
    eff_s[...] = chunked(eff)
    u_s[...] = chunked(delta * act_ref[...])
    length = eff.shape[0] // rows
    sum_ref[...] = jnp.concatenate(
        [jnp.sum(eff[s * length : (s + 1) * length], axis=0, keepdims=True) for s in range(rows)], axis=0
    )
    rate = rate_ref[...] * LOG2E
    ns = rate.shape[0]
    chunks = length // STEPS

    def chunk(k, state):
        state = list(state)
        drive_s[...] = drive_of(bd_ref, u_s, rows, k)
        for t in range(STEPS):
            for s in range(rows):
                at = (s * STEPS + t) * ns
                fade = jnp.exp2(rate * eff_s[s * chunks + k, t : t + 1, :])
                state[s] = fade * state[s] + drive_s[at : at + ns, :]
        return tuple(state)

    zero = jnp.zeros((ns, cb), f32)
    state = lax.fori_loop(0, chunks, chunk, (zero,) * rows)
    for s in range(rows):
        end_ref[s * ns : (s + 1) * ns, :] = state[s]


def scan_kernel(rows, act_ref, delta_ref, z_ref, kill_ref, rate_ref, skip_ref, bd_ref, cd_ref, start_ref,
                y_ref, gated_ref, keep_ref, eff_s, u_s, drive_s, state_s, y_s):
    delta = delta_ref[...]
    cb = delta.shape[1]
    eff_s[...] = chunked(delta + wide(kill_ref[...], cb))
    u_s[...] = chunked(delta * act_ref[...])
    rate = rate_ref[...] * LOG2E
    ns = rate.shape[0]
    length = delta.shape[0] // rows
    chunks = length // STEPS

    def chunk(k, state):
        state = list(state)
        for s in range(rows):
            keep_ref[k, s * ns : (s + 1) * ns, :] = state[s]
        drive_s[...] = drive_of(bd_ref, u_s, rows, k)
        for t in range(STEPS):
            for s in range(rows):
                at = (s * STEPS + t) * ns
                fade = jnp.exp2(rate * eff_s[s * chunks + k, t : t + 1, :])
                state[s] = fade * state[s] + drive_s[at : at + ns, :]
                state_s[at : at + ns, :] = state[s].astype(bf16)
        y = dot(cd_ref[k], state_s[...])
        for s in range(rows):
            y_s[s * chunks + k] = y[s * STEPS : (s + 1) * STEPS]
        return tuple(state)

    lax.fori_loop(0, chunks, chunk, tuple(start_ref[s * ns : (s + 1) * ns, :] for s in range(rows)))
    y = (y_s[...].reshape(delta.shape) + skip_ref[...] * act_ref[...]).astype(bf16)
    y_ref[...] = y
    z = z_ref[...]
    gated_ref[...] = (y.astype(f32) * (z * sigmoid(z))).astype(bf16)


def back_ends_kernel(rows, gg_ref, z_ref, y_ref, delta_ref, kill_ref, rate_ref, cg_ref,
                     gy_ref, gz_ref, end_ref, eff_s, gy_s, push_s):
    z = z_ref[...]
    gg = gg_ref[...]
    sig = sigmoid(z)
    gy = (gg * z * sig).astype(bf16)
    gy_ref[...] = gy
    gz_ref[...] = (gg * y_ref[...].astype(f32) * sig * (1.0 + z * (1.0 - sig))).astype(bf16)
    cb = z.shape[1]
    eff_s[...] = chunked(delta_ref[...] + wide(kill_ref[...], cb))
    gy_s[...] = chunked(gy.astype(f32))
    rate = rate_ref[...] * LOG2E
    ns = rate.shape[0]
    length = z.shape[0] // rows
    chunks = length // STEPS

    def chunk(i, flow):
        k = chunks - 1 - i
        flow = list(flow)
        g16 = tokens_of(gy_s, rows, k).astype(bf16)
        push_s[...] = dot(cg_ref[k], jnp.concatenate([g16, g16], axis=0))
        for t in reversed(range(STEPS)):
            for s in range(rows):
                at = (s * STEPS + t) * ns
                fade = jnp.exp2(rate * eff_s[s * chunks + k, t : t + 1, :])
                flow[s] = fade * (flow[s] + push_s[at : at + ns, :])
        return tuple(flow)

    zero = jnp.zeros((ns, cb), f32)
    flow = lax.fori_loop(0, chunks, chunk, (zero,) * rows)
    for s in range(rows):
        end_ref[s * ns : (s + 1) * ns, :] = flow[s]


def back_kernel(rows, act_ref, delta_ref, gy_ref, kill_ref, rate_ref, skip_ref, dtw_ref, rank_t_ref,
                bd_ref, cg_ref, bt_ref, ones_ref, keep_ref, start_ref,
                gact_ref, gc_ref, gb_ref, grank_ref, gdtw_ref, gbias_ref, grate_ref, gskip_ref,
                eff_s, u_s, gy_s, drive_s, push_s, fade_s, held_s, state_s, grad_s, wa_s, gu_s, gd_s):
    @pl.when(pl.program_id(0) == 0)
    def _():
        gc_ref[...] = jnp.zeros_like(gc_ref)
        gb_ref[...] = jnp.zeros_like(gb_ref)
        grank_ref[...] = jnp.zeros_like(grank_ref)

    delta = delta_ref[...]
    act = act_ref[...]
    gy = gy_ref[...].astype(f32)
    cb = delta.shape[1]
    eff_s[...] = chunked(delta + wide(kill_ref[...], cb))
    u_s[...] = chunked(delta * act)
    gy_s[...] = chunked(gy)
    rate_n = rate_ref[...]
    rate = rate_n * LOG2E
    ns = rate.shape[0]
    length = delta.shape[0] // rows
    chunks = length // STEPS

    def chunk(i, carry):
        flow, total = list(carry[0]), carry[1]
        k = chunks - 1 - i
        g16 = tokens_of(gy_s, rows, k).astype(bf16)
        u16 = tokens_of(u_s, rows, k)
        drive_s[...] = drive_of(bd_ref, u_s, rows, k)
        push_s[...] = dot(cg_ref[k], jnp.concatenate([g16, g16], axis=0))
        state = [keep_ref[k, s * ns : (s + 1) * ns, :] for s in range(rows)]
        for t in range(STEPS):
            for s in range(rows):
                at = (s * STEPS + t) * ns
                fade = jnp.exp2(rate * eff_s[s * chunks + k, t : t + 1, :])
                held = fade * state[s]
                fade_s[at : at + ns, :] = fade
                held_s[at : at + ns, :] = held
                state[s] = held + drive_s[at : at + ns, :]
                state_s[at : at + ns, :] = state[s].astype(bf16)
        gc_ref[k] += dot_nt(g16, state_s[...])
        for t in reversed(range(STEPS)):
            for s in range(rows):
                at = (s * STEPS + t) * ns
                grad = flow[s] + push_s[at : at + ns, :]
                grad_s[at : at + ns, :] = grad.astype(bf16)
                w = grad * held_s[at : at + ns, :]
                step = eff_s[s * chunks + k, t : t + 1, :]
                total = total + w * step
                wa_s[at : at + ns, :] = (w * rate_n).astype(bf16)
                flow[s] = fade_s[at : at + ns, :] * grad
        g_all = grad_s[...]
        gb_ref[k] += dot_nt(u16.astype(bf16), g_all)
        gu = dot(bt_ref[k], g_all)
        gd = dot(ones_ref[...], wa_s[...])
        for s in range(rows):
            gu_s[s * chunks + k] = gu[s * STEPS : (s + 1) * STEPS]
            gd_s[s * chunks + k] = gd[s * STEPS : (s + 1) * STEPS]
        return tuple(flow), total

    first = tuple(start_ref[s * ns : (s + 1) * ns, :] for s in range(rows))
    _, total = lax.fori_loop(0, chunks, chunk, (first, jnp.zeros((ns, cb), f32)))
    grate_ref[...] = total * rate_n
    gu = gu_s[...].reshape(delta.shape)
    gact_ref[...] = gu * delta + skip_ref[...] * gy
    gskip_ref[...] = jnp.sum(gy * act, axis=0, keepdims=True)
    gpre = (gu * act + gd_s[...].reshape(delta.shape)) * (1.0 - jnp.exp(-delta))
    gbias_ref[...] = jnp.sum(gpre, axis=0, keepdims=True)
    gpre16 = gpre.astype(bf16)
    gdtw_ref[...] = dot(rank_t_ref[...], gpre16)
    grank_ref[...] += dot_nt(gpre16, dtw_ref[...])


def conv_back_kernel(rows, x_ref, halo_ref, kern_ref, off_ref, mask_ref, act_ref, gact_ref, gproj_ref,
                     gproj_t_ref, xp_ref, gx_ref, edge_ref, gxp_ref, gkern_ref, goff_ref):
    x = x_ref[...].astype(bf16).astype(f32)
    cb = x.shape[1]
    halo = halo_ref[...].astype(f32)
    kernel = kern_ref[...]
    taps = kernel.shape[0]
    masks = [wide(mask_ref[i], cb) for i in range(taps - 1)]
    pre = conv_sum(x, halo, kernel, off_ref[...], masks, rows)
    sig = sigmoid(pre)
    act16 = act_ref[...].astype(bf16)
    gxp_ref[...] = dot(gproj_t_ref[...], act16)
    g_act = gact_ref[...] + dot(gproj_ref[...], xp_ref[...])
    gpre = g_act * sig * (1.0 + pre * (1.0 - sig))
    goff_ref[...] = jnp.sum(gpre, axis=0, keepdims=True)
    length = x.shape[0] // rows
    place = lax.broadcasted_iota(jnp.int32, (length, cb), 0)
    gk = [jnp.zeros((1, cb), f32) for _ in range(taps)]
    for s in range(rows):
        here = slice(s * length, (s + 1) * length)
        g = gpre[here]
        ext = jnp.concatenate([halo[8 * s : 8 * s + 8], x[here]], axis=0)
        gk[taps - 1] = gk[taps - 1] + jnp.sum(g * x[here], axis=0, keepdims=True)
        gx = kernel[taps - 1 : taps] * g
        edge = jnp.zeros((length, cb), f32)
        for lag in range(1, taps):
            gm = g * masks[lag - 1][here]
            moved = pltpu.roll(ext, lag, 0)[8:]
            j = taps - 1 - lag
            gk[j] = gk[j] + jnp.sum(gm * moved, axis=0, keepdims=True)
            up = pltpu.roll(kernel[j : j + 1] * gm, length - lag, 0)
            inside = place < length - lag
            gx = gx + jnp.where(inside, up, 0.0)
            edge = edge + jnp.where(inside, 0.0, up)
        gx_ref[here, :] = gx
        edge_ref[8 * s : 8 * s + 8, :] = edge[length - 8 :]
    gkern_ref[...] = jnp.concatenate(gk, axis=0)


def col(rows, cb, shift=0):
    return pl.BlockSpec((rows, cb), lambda j: (0, j + shift))


def whole(*shape):
    return pl.BlockSpec(shape, lambda j: (0,) * len(shape))


def call(body, blocks, ins, outs, scratch, args):
    return pl.pallas_call(
        body,
        grid=(blocks,),
        in_specs=ins,
        out_specs=[spec for spec, _, _ in outs],
        out_shape=[jax.ShapeDtypeStruct(shape, kind) for _, shape, kind in outs],
        scratch_shapes=scratch,
        compiler_params=pltpu.CompilerParams(
            dimension_semantics=("arbitrary",), vmem_limit_bytes=VMEM
        ),
    )(*args)


class Mixer:
    def __init__(self, rows, length, channels, ns, rank, taps):
        self.rows, self.length, self.c, self.ns, self.rank, self.taps = rows, length, channels, ns, rank, taps
        self.tokens = rows * length
        self.blocks = channels // CB
        self.chunks = length // STEPS
        self.pairs = rows * STEPS
        self.inner = self.pairs * ns
        self.width = rank + 2 * ns

    def conv(self, projected, halo, p, masks):
        t, c = self.tokens, self.c
        return call(
            functools.partial(conv_kernel, self.rows), self.blocks,
            [col(t, CB), col(8 * self.rows, CB), col(self.taps, CB), col(1, CB), whole(*masks.shape), col(self.width, CB)],
            [(col(t, CB), (t, c), f32), (whole(t, self.width), (t, self.width), f32)],
            [], (projected, halo, p["conv_w"], p["conv_b"], masks, p["xproj"]),
        )

    def maps(self, proj):
        r, b, c = proj[:, : self.rank], proj[:, self.rank : self.rank + self.ns], proj[:, self.rank + self.ns :]
        eye = jnp.eye(self.pairs, dtype=f32)

        def per_chunk(v):
            return (
                v.reshape(self.rows, self.chunks, STEPS, self.ns)
                .transpose(1, 0, 2, 3)
                .reshape(self.chunks, self.pairs, self.ns)
            )

        def tall(v):
            return (per_chunk(v)[:, :, :, None] * eye[None, :, None, :]).reshape(self.chunks, self.inner, self.pairs)

        def flat(v):
            return (per_chunk(v)[:, None, :, :] * eye[None, :, :, None]).reshape(self.chunks, self.pairs, self.inner)

        bh, bl = halves(tall(b))
        ch, cl = halves(tall(c))
        rh, rl = halves(r)
        return dict(
            rank2=jnp.concatenate([rh, rl], axis=1),
            rank_t=rh.T,
            bd=jnp.concatenate([bh, bh, bl], axis=2),
            cg=jnp.concatenate([ch, cl], axis=2),
            bt=flat(b).astype(bf16),
            cd=flat(c).astype(bf16),
        )

    def unmap(self, raw):
        eye = jnp.eye(self.pairs, dtype=f32)
        v = raw.reshape(self.chunks, self.pairs, self.pairs, self.ns)
        v = jnp.sum(v * eye[None, :, :, None], axis=1)
        return v.reshape(self.chunks, self.rows, STEPS, self.ns).transpose(1, 0, 2, 3).reshape(self.tokens, self.ns)

    def scratch3(self):
        return pltpu.VMEM((self.tokens // STEPS, STEPS, CB), f32)

    def wide_scratch(self, kind):
        return pltpu.VMEM((self.inner, CB), kind)

    def ends(self, act, m, p, kill):
        t, c, sn = self.tokens, self.c, self.rows * self.ns
        return call(
            functools.partial(ends_kernel, self.rows), self.blocks,
            [col(t, CB), whole(*m["rank2"].shape), col(self.rank, CB), col(1, CB), whole(*kill.shape), col(self.ns, CB),
             whole(*m["bd"].shape)],
            [(col(t, CB), (t, c), f32), (col(sn, CB), (sn, c), f32), (col(self.rows, CB), (self.rows, c), f32)],
            [self.scratch3(), self.scratch3(), self.wide_scratch(f32)],
            (act, m["rank2"], p["dtproj"], p["dt_b"], kill, p["rate"], m["bd"]),
        )

    def scan(self, act, delta, projected, m, p, kill, start):
        t, c, sn = self.tokens, self.c, self.rows * self.ns
        keep = pl.BlockSpec((self.chunks, sn, CB), lambda j: (0, 0, j))
        return call(
            functools.partial(scan_kernel, self.rows), self.blocks,
            [col(t, CB), col(t, CB), col(t, CB, self.blocks), whole(*kill.shape), col(self.ns, CB), col(1, CB),
             whole(*m["bd"].shape), whole(*m["cd"].shape), col(sn, CB)],
            [(col(t, CB), (t, c), bf16), (col(t, CB), (t, c), bf16), (keep, (self.chunks, sn, c), f32)],
            [self.scratch3(), self.scratch3(), self.wide_scratch(f32), self.wide_scratch(bf16), self.scratch3()],
            (act, delta, projected, kill, p["rate"], p["skip"], m["bd"], m["cd"], start),
        )

    def back_ends(self, gg, projected, y, delta, m, p, kill):
        t, c, sn = self.tokens, self.c, self.rows * self.ns
        return call(
            functools.partial(back_ends_kernel, self.rows), self.blocks,
            [col(t, CB), col(t, CB, self.blocks), col(t, CB), col(t, CB), whole(*kill.shape), col(self.ns, CB),
             whole(*m["cg"].shape)],
            [(col(t, CB), (t, c), bf16), (col(t, CB), (t, c), bf16), (col(sn, CB), (sn, c), f32)],
            [self.scratch3(), self.scratch3(), self.wide_scratch(f32)],
            (gg, projected, y, delta, kill, p["rate"], m["cg"]),
        )

    def back(self, act, delta, gy, m, p, kill, keep, start):
        t, c, sn, ns = self.tokens, self.c, self.rows * self.ns, self.ns
        kept = pl.BlockSpec((self.chunks, sn, CB), lambda j: (0, 0, j))
        raw = (self.chunks, self.pairs, self.inner)
        ones = jnp.repeat(jnp.eye(self.pairs, dtype=bf16), ns, axis=1)
        return call(
            functools.partial(back_kernel, self.rows), self.blocks,
            [col(t, CB), col(t, CB), col(t, CB), whole(*kill.shape), col(ns, CB), col(1, CB), col(self.rank, CB),
             whole(*m["rank_t"].shape), whole(*m["bd"].shape), whole(*m["cg"].shape), whole(*m["bt"].shape),
             whole(*ones.shape), kept, col(sn, CB)],
            [(col(t, CB), (t, c), f32), (whole(*raw), raw, f32), (whole(*raw), raw, f32),
             (whole(t, self.rank), (t, self.rank), f32), (col(self.rank, CB), (self.rank, c), f32),
             (col(1, CB), (1, c), f32), (col(ns, CB), (ns, c), f32), (col(1, CB), (1, c), f32)],
            [self.scratch3()] * 3 + [self.wide_scratch(f32)] * 4 + [self.wide_scratch(bf16)] * 3 + [self.scratch3()] * 2,
            (act, delta, gy, kill, p["rate"], p["skip"], p["dtproj"], m["rank_t"], m["bd"], m["cg"], m["bt"], ones,
             keep, start),
        )

    def conv_back(self, projected, halo, p, masks, act, gact, gproj):
        t, c = self.tokens, self.c
        g16 = gproj.astype(bf16)
        return call(
            functools.partial(conv_back_kernel, self.rows), self.blocks,
            [col(t, CB), col(8 * self.rows, CB), col(self.taps, CB), col(1, CB), whole(*masks.shape), col(t, CB),
             col(t, CB), whole(t, self.width), whole(self.width, t), col(self.width, CB)],
            [(col(t, CB), (t, c), f32), (col(8 * self.rows, CB), (8 * self.rows, c), f32),
             (col(self.width, CB), (self.width, c), f32), (col(self.taps, CB), (self.taps, c), f32),
             (col(1, CB), (1, c), f32)],
            [], (projected, halo, p["conv_w"], p["conv_b"], masks, act, gact, g16, g16.T, p["xproj"]),
        )


def carried_in(ends, sums, rate, axis, backward):
    n = lax.axis_size(axis)
    rows = sums.shape[0]
    ns = rate.shape[0]

    def fade(total):
        return jnp.exp(total[:, None, :] * rate[None])

    def moved(v, shift):
        if backward:
            pairs = [(i, i - shift) for i in range(shift, n)]
        else:
            pairs = [(i, i + shift) for i in range(n - shift)]
        return lax.ppermute(v, axis, pairs)

    def shifted(e, s, shift):
        return moved(e.astype(bf16), shift).astype(f32), moved(s, shift)

    ends = ends.reshape(rows, ns, -1)
    ends, sums = shifted(ends, sums, 1)
    shift = 1
    while shift < n - 1:
        e, s = shifted(ends, sums, shift)
        ends = fade(sums) * e + ends
        sums = sums + s
        shift *= 2
    return ends.reshape(rows * ns, -1)


def body(
    tokens, boundaries, norm_gain, in_weight, out_weight, conv_weight, conv_bias, xproj_weight,
    dtproj_weight, dt_bias, decay_log, skip_gain, cotangent,
):
    rows, length, d = tokens.shape
    layers = norm_gain.shape[0]
    both = ("rows", "bytes")
    n = rows * length
    place = lax.axis_index("bytes") * length + jnp.arange(length, dtype=jnp.int32)
    reached = boundaries[:, None, :] <= place[None, :, None]
    starts = jnp.max(jnp.where(reached, boundaries[:, None, :], 0), axis=2)
    renewed = jnp.any(boundaries[:, None, :] == place[None, :, None], axis=2)
    kill = jnp.broadcast_to(jnp.where(renewed, KILL, 0.0).reshape(n, 1), (n, 128)).astype(f32)
    taps = conv_weight.shape[1]
    masks = jnp.stack(
        [
            jnp.broadcast_to((place[None, :] - lag >= starts).astype(f32).reshape(n, 1), (n, 128))
            for lag in range(1, taps)
        ]
    )
    half = jnp.concatenate([xproj_weight.transpose(0, 2, 1), dtproj_weight], axis=1)
    full = jnp.concatenate(
        [conv_weight, conv_bias[:, None], dt_bias[:, None], skip_gain[:, None], -jnp.exp(decay_log)], axis=1
    )
    half = lax.all_gather(half, "bytes", axis=2, tiled=True)
    full = lax.all_gather(full, "bytes", axis=2, tiled=True)
    ns = decay_log.shape[1]
    rank = dtproj_weight.shape[1]
    width = xproj_weight.shape[2]
    channels = full.shape[2]
    mixer = Mixer(rows, length, channels, ns, rank, taps)
    params = []
    for i in range(layers):
        params.append(
            dict(
                xproj=half[i, :width], dtproj=half[i, width:], conv_w=full[i, :taps], conv_b=full[i, taps : taps + 1],
                dt_b=full[i, taps + 1 : taps + 2], skip=full[i, taps + 2 : taps + 3], rate=full[i, taps + 3 :],
            )
        )
    weights = [
        (
            lax.all_gather(in_weight[i], both, axis=0, tiled=True),
            lax.all_gather(out_weight[i], both, axis=0, tiled=True),
        )
        for i in range(layers)
    ]
    size = lax.axis_size("bytes")
    ahead = [(i, i + 1) for i in range(size - 1)]
    behind = [(i + 1, i) for i in range(size - 1)]
    current = tokens.astype(f32).reshape(n, d)
    saved = []
    for i in range(layers):
        p = params[i]
        in_full, out_full = weights[i]
        normed = (
            current * lax.rsqrt(jnp.mean(current * current, axis=-1, keepdims=True) + norm_eps) * norm_gain[i]
        ).astype(bf16)
        projected = dot_nt(normed, in_full)
        tail = projected.reshape(rows, length, -1)[:, length - 8 :, :channels].astype(bf16)
        halo = lax.ppermute(tail, "bytes", ahead).reshape(8 * rows, channels)
        act, proj = mixer.conv(projected, halo, p, masks)
        m = mixer.maps(proj)
        delta, end, total = mixer.ends(act, m, p, kill)
        start = carried_in(end, total, p["rate"], "bytes", False)
        y, gated, keep = mixer.scan(act, delta, projected, m, p, kill, start)
        saved.append((current, normed, projected, halo, act, m, delta, total, y, gated, keep))
        current = current + dot(gated, out_full)
    flowing = cotangent.astype(f32).reshape(n, d)
    big, small, gains = [], [], []
    for i in reversed(range(layers)):
        p = params[i]
        in_full, out_full = weights[i]
        before, normed, projected, halo, act, m, delta, total, y, gated, keep = saved[i]
        down = flowing.astype(bf16)
        grad_out = lax.dot_general(gated, down, (((0,), (0,)), ((), ())), preferred_element_type=f32).astype(bf16)
        gg = dot_nt(down, out_full)
        gy, gz, gend = mixer.back_ends(gg, projected, y, delta, m, p, kill)
        gstart = carried_in(gend, total, p["rate"], "bytes", True)
        gact, graw_c, graw_b, grank, gdtw, gbias, grate, gskip = mixer.back(
            act, delta, gy, m, p, kill, keep, gstart
        )
        gproj = jnp.concatenate([grank, mixer.unmap(graw_b), mixer.unmap(graw_c)], axis=1)
        gx, edge, gxp, gkern, goff = mixer.conv_back(projected, halo, p, masks, act, gact, gproj)
        late = lax.ppermute(edge.astype(bf16), "bytes", behind).astype(f32).reshape(rows, 8, channels)
        gx = (
            (gx.reshape(rows, length, channels) + jnp.pad(late, ((0, 0), (length - 8, 0), (0, 0))))
            .reshape(n, channels)
            .astype(bf16)
        )
        mixed = jnp.concatenate([gx, gz], axis=1)
        grad_in = lax.dot_general(mixed, normed, (((0,), (0,)), ((), ())), preferred_element_type=f32).astype(bf16)
        gn = dot(mixed, in_full)
        inv = lax.rsqrt(jnp.mean(before * before, axis=-1, keepdims=True) + norm_eps)
        scaled = before * inv
        gains.append(jnp.sum(gn * scaled, axis=0))
        gs = gn * norm_gain[i]
        flowing = flowing + inv * (gs - scaled * jnp.mean(gs * scaled, axis=-1, keepdims=True))
        big.append(
            (
                lax.psum_scatter(grad_in, both, scatter_dimension=0, tiled=True).astype(f32),
                lax.psum_scatter(grad_out, both, scatter_dimension=0, tiled=True).astype(f32),
            )
        )
        small.append(jnp.concatenate([gxp, gdtw, grate, gkern, goff, gbias, gskip], axis=0))
    big, small, gains = big[::-1], small[::-1], gains[::-1]
    packed = jnp.stack(small).astype(bf16)
    packed = lax.psum_scatter(packed, "bytes", scatter_dimension=2, tiled=True)
    packed = lax.psum(packed, "rows").astype(f32)
    cuts = [width, rank, ns, taps, 1, 1, 1]
    parts, at = [], 0
    for cut in cuts:
        parts.append(packed[:, at : at + cut])
        at += cut
    gain_total = lax.psum(jnp.stack(gains), both)
    return (
        current.reshape(rows, length, d),
        flowing.reshape(rows, length, d),
        gain_total,
        jnp.stack([b[0] for b in big]),
        jnp.stack([b[1] for b in big]),
        parts[3],
        parts[4][:, 0],
        parts[0].transpose(0, 2, 1),
        parts[1],
        parts[5][:, 0],
        parts[2],
        parts[6][:, 0],
    )


def solution(mesh):
    split = P("rows", "bytes", None)
    shared = P(None, ("rows", "bytes"), None)
    in_specs = (
        split, P("rows", None), P(), shared, shared, P(None, None, "bytes"), P(None, "bytes"),
        P(None, "bytes", None), P(None, None, "bytes"), P(None, "bytes"), P(None, None, "bytes"),
        P(None, "bytes"), split,
    )
    out_specs = (
        split, split, P(), shared, shared, P(None, None, "bytes"), P(None, "bytes"), P(None, "bytes", None),
        P(None, None, "bytes"), P(None, "bytes"), P(None, None, "bytes"), P(None, "bytes"),
    )
    return jax.shard_map(body, mesh=mesh, in_specs=in_specs, out_specs=out_specs, check_vma=False)
```

profile of v0, /device:TPU:0, one launch (start us, length us, event | category | flops | bytes accessed | tf_op | source)
XLA Modules:
  0.0 1412.5 jit_solution(13490252654153001014)
XLA Ops:
  19.1 17.4 %all_gather.19 = f32[2,23,2048]{2,1,0:T(8,128)S(1)} all-gather(f32[2,23,256]{2,1,0:T(8,128)S(1)} %concatenate.46), channel_id=1, replica_groups=mesh['rows'=4,'bytes'=8] {'bytes'}, dimensions={2}, use_global_device_ids=true | all-gather | bytes 423936 | tf_op jit(solution)/shard_map/all_gather | solution.py:508
  42.8 78.0 %all-gather.12.cloned.1.call-done = bf16[1,4096,1024]{2,1,0:T(8,128)(2,1)} async-done(((bf16[1,128,1024]{2,1,0:T(8,128)(2,1)}), bf16[1,4096,1024]{2,1,0:T(8,128)(2,1)}) %all-gather.12.cloned.1.call-update) | async-done | bytes 8388624 | tf_op jit(solution)/shard_map/all_gather | solution.py:524
  120.8 7.8 fusion.53
  132.7 5.8 shard_map.220
  147.2 24.6 %shard_map.221 = (f32[256,2048]{1,0:T(8,128)S(1)}, f32[32,2048]{1,0:T(8,128)S(1)}, f32[2,2048]{1,0:T(2,128)S(1)}) custom-call(f32[256,2048]{1,0:T(8,128)S(1)} %get-tuple-element.60.act_ref, bf16[256,128]{1,0:T(8,128)(2,1)S(1)} %copy-done.62, bf16[64,2048]{1,0:T(8,128)(2,1)S(1)} %copy-done.25, f32[1,2048]{1,0:T(1,128)S(1)} %copy-done.77, ...), custom_call_target="tpu_custom_call" | custom-call | tf_op jit(solution)/shard_map/pallas_call | solution.py:315
  177.5 6.2 collective-permute-start.5
  215.2 43.7 %shard_map.222 = (bf16[256,2048]{1,0:T(8,128)(2,1)S(1)}, bf16[256,2048]{1,0:T(8,128)(2,1)S(1)}, f32[16,32,2048]{2,1,0:T(8,128)}) custom-call(f32[256,2048]{1,0:T(8,128)S(1)} %get-tuple-element.60.act_ref, f32[256,2048]{1,0:T(8,128)} %copy-done.4, f32[256,4096]{1,0:T(8,128)} %get-tuple-element.170.x_ref.z_ref, f32[256,128]{1,0:T(8,128)S(1)} %broadcast_in_dim.36.kill_ref, ...), custom_call_target="tpu_custom_call" | custom-call | tf_op jit(solution)/shard_map/pallas_call | solution.py:315
  265.3 8.1 fusion.54
  276.1 5.8 shard_map.223
  303.1 24.6 %shard_map.224 = (f32[256,2048]{1,0:T(8,128)S(1)}, f32[32,2048]{1,0:T(8,128)S(1)}, f32[2,2048]{1,0:T(2,128)S(1)}) custom-call(f32[256,2048]{1,0:T(8,128)S(1)} %get-tuple-element.66.act_ref, bf16[256,128]{1,0:T(8,128)(2,1)S(1)} %copy-done.61, bf16[64,2048]{1,0:T(8,128)(2,1)S(1)} %copy-done.27, f32[1,2048]{1,0:T(1,128)S(1)} %copy-done.76, ...), custom_call_target="tpu_custom_call" | custom-call | tf_op jit(solution)/shard_map/pallas_call | solution.py:315
  329.1 9.6 collective-permute-start.12
  339.6 5.5 collective-permute-start.13
  366.8 5.9 collective-permute-start.15
  382.7 43.8 %shard_map.225 = (bf16[256,2048]{1,0:T(8,128)(2,1)S(1)}, bf16[256,2048]{1,0:T(8,128)(2,1)S(1)}, f32[16,32,2048]{2,1,0:T(8,128)}) custom-call(f32[256,2048]{1,0:T(8,128)S(1)} %get-tuple-element.66.act_ref, f32[256,2048]{1,0:T(8,128)} %copy-done.5, f32[256,4096]{1,0:T(8,128)} %get-tuple-element.174.x_ref.z_ref, f32[256,128]{1,0:T(8,128)S(1)} %broadcast_in_dim.36.kill_ref, ...), custom_call_target="tpu_custom_call" | custom-call | tf_op jit(solution)/shard_map/pallas_call | solution.py:315
  427.5 26.9 %shard_map.226 = (bf16[256,2048]{1,0:T(8,128)(2,1)S(1)}, bf16[256,2048]{1,0:T(8,128)(2,1)S(1)}, f32[32,2048]{1,0:T(8,128)S(1)}) custom-call(f32[256,2048]{1,0:T(8,128)} %fusion.8.gg_ref, f32[256,4096]{1,0:T(8,128)} %get-tuple-element.174.x_ref.z_ref, bf16[256,2048]{1,0:T(8,128)(2,1)S(1)} %get-tuple-element.72.y_ref, f32[256,2048]{1,0:T(8,128)} %copy-done.5, ...), custom_call_target="tpu_custom_call" | custom-call | tf_op jit(solution)/shard_map/pallas_call | solution.py:315
  476.7 6.2 collective-permute-done.18
  492.7 57.5 %shard_map.227 = (f32[256,2048]{1,0:T(8,128)}, f32[16,16,256]{2,1,0:T(8,128)S(1)}, f32[16,16,256]{2,1,0:T(8,128)S(1)}, f32[256,64]{1,0:T(8,128)S(1)}, f32[64,204...) custom-call(f32[256,2048]{1,0:T(8,128)} %copy-done.2, ...), custom_call_target="tpu_custom_call" | custom-call | tf_op jit(solution)/shard_map/pallas_call | solution.py:315
  563.7 7.6 shard_map.228
  580.2 7.1 multiply_reduce_fusion
  590.4 27.0 %shard_map.229 = (bf16[256,2048]{1,0:T(8,128)(2,1)S(1)}, bf16[256,2048]{1,0:T(8,128)(2,1)S(1)}, f32[32,2048]{1,0:T(8,128)S(1)}) custom-call(f32[256,2048]{1,0:T(8,128)} %fusion.12.gg_ref, f32[256,4096]{1,0:T(8,128)} %get-tuple-element.170.x_ref.z_ref, bf16[256,2048]{1,0:T(8,128)(2,1)S(1)} %copy-done.38, f32[256,2048]{1,0:T(8,128)} %copy-done.4, ...), custom_call_target="tpu_custom_call" | custom-call | tf_op jit(solution)/shard_map/pallas_call | solution.py:315
  641.6 6.4 collective-permute-done.26
  656.7 57.5 %shard_map.230 = (f32[256,2048]{1,0:T(8,128)}, f32[16,16,256]{2,1,0:T(8,128)S(1)}, f32[16,16,256]{2,1,0:T(8,128)S(1)}, f32[256,64]{1,0:T(8,128)S(1)}, f32[64,204...) custom-call(f32[256,2048]{1,0:T(8,128)} %copy-done, ...), custom_call_target="tpu_custom_call" | custom-call | tf_op jit(solution)/shard_map/pallas_call | solution.py:315
  720.9 7.7 shard_map.231
  735.9 34.0 %reduce-scatter.14.cloned.1.call-done = bf16[2,183,256]{2,1,0:T(8,128)(2,1)} async-done(((bf16[2,183,2048]{2,1,0:T(8,128)(2,1)}), bf16[2,183,256]{2,1,0:T(8,128)(2,1)}) %reduce-scatter.14.cloned.1.call-update) | async-done | bytes 187408 | tf_op jit(solution)/shard_map/reduce_scatter | solution.py:589
  779.6 7.0 convolution_convert_fusion
  791.1 7.1 convolution_convert_fusion.1
  804.2 6.0 multiply_reduce_fusion.1
  810.2 38.8 %psum.14 = f32[2,1024]{1,0:T(2,128)} all-reduce(f32[2,1024]{1,0:T(2,128)S(1)} %pad_maximum_fusion.17), channel_id=1, replica_groups=mesh['rows'=4,'bytes'=8] {'rows','bytes'}, use_global_device_ids=true, to_apply=%region_12.13 | all-reduce | flops 2048 | bytes 16384 | tf_op jit(solution)/shard_map/psum | solution.py:596
  858.7 99.8 %reduce-scatter.12.cloned.1.call-done = bf16[64,1024]{1,0:T(8,128)(2,1)} async-done(((bf16[2048,1024]{1,0:T(8,128)(2,1)}), bf16[64,1024]{1,0:T(8,128)(2,1)}) %reduce-scatter.12.cloned.1.call-update) | async-done | bytes 131088 | tf_op jit(solution)/shard_map/reduce_scatter | solution.py:583
  958.4 141.8 %reduce-scatter.10.cloned.1.call-done = bf16[64,1024]{1,0:T(8,128)(2,1)} async-done(((bf16[2048,1024]{1,0:T(8,128)(2,1)}), bf16[64,1024]{1,0:T(8,128)(2,1)}) %reduce-scatter.10.cloned.1.call-update) | async-done | bytes 131088 | tf_op jit(solution)/shard_map/reduce_scatter | solution.py:583
  1102.0 149.5 %reduce-scatter.8.cloned.1.call-done = bf16[128,1024]{1,0:T(8,128)(2,1)} async-done(((bf16[4096,1024]{1,0:T(8,128)(2,1)}), bf16[128,1024]{1,0:T(8,128)(2,1)}) %reduce-scatter.8.cloned.1.call-update) | async-done | bytes 262160 | tf_op jit(solution)/shard_map/reduce_scatter | solution.py:582
  1251.5 151.9 %reduce-scatter.6.cloned.1.call-done = bf16[128,1024]{1,0:T(8,128)(2,1)} async-done(((bf16[4096,1024]{1,0:T(8,128)(2,1)}), bf16[128,1024]{1,0:T(8,128)(2,1)}) %reduce-scatter.6.cloned.1.call-update) | async-done | bytes 262160 | tf_op jit(solution)/shard_map/reduce_scatter | solution.py:582
  (534 shorter events, 269.7 us)
Async XLA Ops:
  7.2 33.7 %all-gather.10.cloned.1.call-start = ((), (), s32[]{:S(2)}) async-start(), calls=%async_computation.5 | async-start | bytes 1474560 | tf_op jit(solution)/shard_map/all_gather | solution.py:507
  8.9 111.9 %all-gather.12.cloned.1.call-start = ((), (), s32[]{:S(2)}) async-start(), calls=%async_computation.12 | async-start | bytes 8650752 | tf_op jit(solution)/shard_map/all_gather | solution.py:524
  10.8 250.1 %all-gather.14.cloned.1.call-start = ((), (), s32[]{:S(2)}) async-start(), calls=%async_computation.13 | async-start | bytes 4325376 | tf_op jit(solution)/shard_map/all_gather | solution.py:525
  12.6 252.6 %all-gather.16.cloned.1.call-start = ((), (), s32[]{:S(2)}) async-start(), calls=%async_computation.14 | async-start | bytes 8650752 | tf_op jit(solution)/shard_map/all_gather | solution.py:524
  13.2 345.4 %all-gather.18.cloned.1.call-start = ((), (), s32[]{:S(2)}) async-start(), calls=%async_computation.15 | async-start | bytes 4325376 | tf_op jit(solution)/shard_map/all_gather | solution.py:525
  13.8 756.1 %reduce-scatter.14.cloned.1.call-start = ((), (), s32[]{:S(2)}) async-start(), calls=%async_computation.10 | async-start | bytes 1695744 | tf_op jit(solution)/shard_map/reduce_scatter | solution.py:589
  177.5 11.6 collective-permute-start.5
  183.7 5.3 collective-permute-start.1
  190.5 16.4 %collective-permute-start.6 = (bf16[2,16,2048]{2,1,0:T(8,128)(2,1)}, bf16[2,16,2048]{2,1,0:T(8,128)(2,1)}, u32[]{:S(2)}, u32[]{:S(2)}) collective-permute-start(bf16[2,16,2048]{2,1,0:T(8,128)(2,1)} %fusion.28), channel_id=1, source_target_pairs={{0,2},{1,3},{2,4},{3,5},{4,6},{5,7},{8,10},{9,11},{10,12},{11,13},... | collective-permute-start | bytes 393224 | tf_op jit(solution)/shard_map/ppermute | solution.py:467
  195.3 8.1 collective-permute-start.2
  204.1 7.6 collective-permute-start.3
  208.1 5.9 collective-permute-start.7
  329.1 10.5 collective-permute-start.12
  339.6 13.7 collective-permute-start.13
  350.4 13.3 collective-permute-start.10
  354.7 10.4 collective-permute-start.14
  366.8 12.4 collective-permute-start.15
  458.6 7.6 collective-permute-start.20
  459.9 6.3 collective-permute-start.16
  466.3 7.5 collective-permute-start.21
  473.9 11.7 collective-permute-start.22
  475.2 7.7 collective-permute-start.18
  623.2 8.1 collective-permute-start.28
  624.5 6.8 collective-permute-start.24
  631.4 7.5 collective-permute-start.29
  639.0 12.7 collective-permute-start.30
  640.3 7.7 collective-permute-start.26
  735.8 114.5 %all-reduce.4.cloned.1.call-start = ((), (), s32[]{:S(2)}) async-start(), calls=%async_computation.11 | async-start | bytes 376832 | tf_op jit(solution)/shard_map/psum | solution.py:590
  769.9 188.5 %reduce-scatter.12.cloned.1.call-start = ((), (), s32[]{:S(2)}) async-start(), calls=%async_computation.9 | async-start | bytes 4325376 | tf_op jit(solution)/shard_map/reduce_scatter | solution.py:583
  773.3 327.0 %reduce-scatter.10.cloned.1.call-start = ((), (), s32[]{:S(2)}) async-start(), calls=%async_computation.8 | async-start | bytes 4325376 | tf_op jit(solution)/shard_map/reduce_scatter | solution.py:583
  778.1 473.4 %reduce-scatter.8.cloned.1.call-start = ((), (), s32[]{:S(2)}) async-start(), calls=%async_computation.7 | async-start | bytes 8650752 | tf_op jit(solution)/shard_map/reduce_scatter | solution.py:582
  786.6 616.8 %reduce-scatter.6.cloned.1.call-start = ((), (), s32[]{:S(2)}) async-start(), calls=%async_computation.6 | async-start | bytes 8650752 | tf_op jit(solution)/shard_map/reduce_scatter | solution.py:582
  (157 other events, 2432.8 us)
Sparse Core Ops, SparseCore 0:
  10.2 30.3 all-gather.9
  44.2 76.5 all-gather.11
  123.8 61.0 all-gather.13
  188.4 76.7 all-gather.15
  268.0 60.8 all-gather.17
  735.9 33.9 reduce-scatter.13
  772.8 40.5 all-reduce.3
  815.8 142.6 reduce-scatter.11
  960.8 139.3 reduce-scatter.9
  1102.5 148.9 reduce-scatter.7
  1253.9 149.4 reduce-scatter.5
where the time goes:
time: 1430 us; the launch traced here: 1410 us
  waiting for transfers between devices  704 us (49%)
  Pallas kernels  333 us (23%)
  local copies, waits for them, and re-layouts  110 us (8%)
  starting transfers between devices  87.4 us (6%)
  matrix products  66.3 us (5%)
  blocking collectives  56.2 us (4%)
  other arithmetic  39.8 us (3%)
  between operations  16 us (1%)
    pallas_call x12, Pallas kernels, call(): pl.pallas_call(body, grid=(blocks,), in_specs=ins, out_specs=[spec for sp...  333 us
    reduce_scatter x2, waiting for transfers between devices, body(): lax.psum_scatter(grad_in, both, scatter_dimension=0, tiled=True).astype(f32)  301 us
    reduce_scatter x2, waiting for transfers between devices, body(): lax.psum_scatter(grad_out, both, scatter_dimension=0, tiled=True)  242 us
    ppermute x28, starting transfers between devices, moved(): return lax.ppermute(v, axis, pairs)  79.6 us
    all_gather x2, waiting for transfers between devices, body(): lax.all_gather(in_weight[i], both, axis=0, tiled=True)  78 us
    unnamed x295, local copies, waits for them, and re-layouts  51.7 us
    ppermute x28, waiting for transfers between devices, moved(): return lax.ppermute(v, axis, pairs)  45.6 us
    psum x1, blocking collectives, body(): gain_total = lax.psum(jnp.stack(gains), both)  38.8 us
  transfers between devices with their start and end apart: 43, of which 24 were waited for; matrix products, arithmetic and copies ran while one was open for 9% of the time, Pallas kernels for 7%

commit v1 on v0

v1 whole, which is shorter than its diff:
```python
import functools

import jax
import jax.numpy as jnp
from jax import lax
from jax.experimental import pallas as pl
from jax.experimental.pallas import tpu as pltpu
from jax.sharding import PartitionSpec as P

norm_eps = 1e-05
f32 = jnp.float32
bf16 = jnp.bfloat16
STEPS = 8
CB = 256
CB_ENDS = 512
CB_SCAN = 512
CB_BACK = 512
KILL = 1e30
LOG2E = 1.4426950408889634
VMEM = 58 * 2**20
FORWARD_ONE = (8, 15, 16, 17, 18, 18, 19, 20, 21)
FORWARD_EARLY = (8, 16, 17, 19, 20, 20, 20, 22, 23)
BACKWARD_STEPS = (0, 2, 4, 4, 4, 4, 4, 5, 6, 7, 8)

NT = (((1,), (1,)), ((), ()))


def dot(a, b):
    return jnp.dot(a, b, preferred_element_type=f32)


def dot_nt(a, b):
    return lax.dot_general(a, b, NT, preferred_element_type=f32)


def halves(v):
    high = v.astype(bf16)
    return high, (v - high.astype(f32)).astype(bf16)


def wide(v, width):
    return jnp.concatenate([v] * (width // v.shape[1]), axis=1)


def sigmoid(v):
    return 1.0 / (1.0 + jnp.exp(-v))


def conv_sum(x, halo, kernel, offset, masks, rows):
    length = x.shape[0] // rows
    taps = kernel.shape[0]
    outs = []
    for s in range(rows):
        ext = jnp.concatenate([halo[8 * s : 8 * s + 8], x[s * length : (s + 1) * length]], axis=0)
        total = offset + kernel[taps - 1 : taps] * ext[8:]
        for lag in range(1, taps):
            moved = pltpu.roll(ext, lag, 0)[8:]
            m = masks[lag - 1][s * length : (s + 1) * length]
            total = total + kernel[taps - 1 - lag : taps - lag] * moved * m
        outs.append(total)
    return jnp.concatenate(outs, axis=0)


class Packed:
    def __init__(self, rank, ns, taps):
        self.rank, self.ns, self.taps = rank, ns, taps
        self.width = rank + 2 * ns

    def rate(self, ref):
        return ref.at[0 : self.ns]

    def kernel(self, ref):
        return ref.at[self.ns : self.ns + self.taps]

    def row(self, ref, i):
        return ref.at[self.ns + self.taps + i : self.ns + self.taps + i + 1]

    def offset(self, ref):
        return self.row(ref, 0)

    def bias(self, ref):
        return self.row(ref, 1)

    def skip(self, ref):
        return self.row(ref, 2)

    def xproj(self, ref):
        return ref.at[0 : self.width]

    def dtproj(self, ref):
        return ref.at[self.width : self.width + self.rank]


def maps_part(rows, rank, ns, proj, rank2_ref, rank_t_ref, bb_ref, cc_ref, cd_ref):
    tokens = proj.shape[0]
    high, low = halves(proj[:, :rank])
    rank2_ref[...] = jnp.concatenate([high, low], axis=1)
    turned = proj.T
    rank_t_ref[...] = turned[:rank].astype(bf16)
    per = tokens // rows // STEPS
    for s in range(rows):
        for k in range(per):
            for t in range(STEPS):
                tok = (s * per + k) * STEPS + t
                at = ((k * rows + s) * STEPS + t) * ns
                bb_ref[at : at + ns, :] = jnp.broadcast_to(turned[rank : rank + ns, tok : tok + 1], (ns, 128))
                cc_ref[at : at + ns, :] = jnp.broadcast_to(turned[rank + ns :, tok : tok + 1], (ns, 128))
    inner = cd_ref.shape[-1]
    tile = (
        lax.broadcasted_iota(jnp.int32, (ns, inner), 0) == lax.broadcasted_iota(jnp.int32, (ns, inner), 1) % ns
    ).astype(bf16)
    spread = dot(proj[:, rank + ns :].astype(bf16), tile)
    tok = lax.broadcasted_iota(jnp.int32, (tokens, inner), 0)
    own = (tok // (tokens // rows)) * STEPS + tok % STEPS
    cd = jnp.where(own == lax.broadcasted_iota(jnp.int32, (tokens, inner), 1) // ns, spread, 0.0)
    cd_ref[...] = cd.reshape(cd_ref.shape)


def conv_part(rows, x, halo, kern_ref, off_ref, mask_ref, xp_ref, proj_s):
    cb = x.shape[1]
    masks = [wide(mask_ref[i], cb) for i in range(mask_ref.shape[0])]
    pre = conv_sum(x, halo, kern_ref[...], off_ref[...], masks, rows)
    act = pre * sigmoid(pre)
    high, low = halves(act)
    weight = xp_ref[...]
    proj_s[...] += dot_nt(high, weight) + dot_nt(low, weight)
    return act


def conv_kernel(rows, sizes, x_ref, halo_ref, kern_ref, off_ref, mask_ref, xp_ref,
                act_ref, rank2_ref, rank_t_ref, bb_ref, cc_ref, cd_ref, proj_s):
    block = pl.program_id(0)

    @pl.when(block == 0)
    def _():
        proj_s[...] = jnp.zeros_like(proj_s)

    act_ref[...] = conv_part(
        rows, x_ref[...].astype(bf16).astype(f32), halo_ref[...].astype(f32), kern_ref, off_ref, mask_ref, xp_ref, proj_s
    )

    @pl.when(block == pl.num_programs(0) - 1)
    def _():
        maps_part(rows, *sizes, proj_s[...], rank2_ref, rank_t_ref, bb_ref, cc_ref, cd_ref)


def step_sizes(rank2_ref, dtw_ref, bias_ref):
    weight = dtw_ref[...]
    pre = dot(rank2_ref[...], jnp.concatenate([weight, weight], axis=0)) + bias_ref[...]
    return jnp.maximum(pre, 0.0) + jnp.log1p(jnp.exp(-jnp.abs(pre)))


def chunked(v):
    return v.reshape(v.shape[0] // STEPS, STEPS, v.shape[1])


def tile_rows(ref, k, at, ns, inner, cb):
    v = ref[pl.ds(pl.multiple_of(k * inner, inner) + at, ns), :]
    return jnp.concatenate([v] * (cb // v.shape[1]), axis=1)


def lane_sum(v):
    out = v[:, :128]
    for i in range(1, v.shape[1] // 128):
        out = out + v[:, 128 * i : 128 * (i + 1)]
    return out


def ends_part(rows, act, rank2_ref, dtw_ref, bias_ref, kill_ref, rate_ref, bb_ref, eff_s, u_s):
    delta = step_sizes(rank2_ref, dtw_ref, bias_ref)
    cb = delta.shape[1]
    eff = delta + wide(kill_ref[...], cb)
    eff_s[...] = chunked(eff)
    u_s[...] = chunked(delta * act)
    length = eff.shape[0] // rows
    sums = jnp.concatenate(
        [jnp.sum(eff[s * length : (s + 1) * length], axis=0, keepdims=True) for s in range(rows)], axis=0
    )
    rate = rate_ref[...] * LOG2E
    ns = rate.shape[0]
    chunks = length // STEPS
    inner = rows * STEPS * ns

    def chunk(k, state):
        state = list(state)
        for t in range(STEPS):
            for s in range(rows):
                fade = jnp.exp2(rate * eff_s[s * chunks + k, t : t + 1, :])
                drive = u_s[s * chunks + k, t : t + 1, :] * tile_rows(bb_ref, k, (s * STEPS + t) * ns, ns, inner, cb)
                state[s] = fade * state[s] + drive
        return tuple(state)

    zero = jnp.zeros((ns, cb), f32)
    state = lax.fori_loop(0, chunks, chunk, (zero,) * rows)
    return delta, sums, jnp.concatenate(state, axis=0)


def scan_part(rows, delta, act, z, kill_ref, rate_ref, skip_ref, bb_ref, cd_ref, start,
              y_ref, gated_ref, keep_ref, eff_s, u_s, sa, sb, y_s):
    cb = delta.shape[1]
    eff_s[...] = chunked(delta + wide(kill_ref[...], cb))
    u_s[...] = chunked(delta * act)
    rate = rate_ref[...] * LOG2E
    ns = rate.shape[0]
    length = delta.shape[0] // rows
    chunks = length // STEPS
    inner = rows * STEPS * ns

    def scan(k, state, held):
        state = list(state)
        for s in range(rows):
            keep_ref[k, s * ns : (s + 1) * ns, :] = state[s]
        for t in range(STEPS):
            for s in range(rows):
                at = (s * STEPS + t) * ns
                fade = jnp.exp2(rate * eff_s[s * chunks + k, t : t + 1, :])
                drive = u_s[s * chunks + k, t : t + 1, :] * tile_rows(bb_ref, k, at, ns, inner, cb)
                state[s] = fade * state[s] + drive
                held[at : at + ns, :] = state[s].astype(bf16)
        return tuple(state)

    def leave(k, held):
        left = jnp.concatenate([cd_ref[s * chunks + k] for s in range(rows)], axis=0).astype(bf16)
        y = dot(left, held[...])
        for s in range(rows):
            y_s[s * chunks + k] = y[s * STEPS : (s + 1) * STEPS]

    sb[...] = jnp.zeros_like(sb)

    def two(i, state):
        k = 2 * i
        leave(jnp.maximum(k - 1, 0), sb)
        state = scan(k, state, sa)
        leave(k, sa)
        return scan(k + 1, state, sb)

    lax.fori_loop(0, chunks // 2, two, tuple(start[s * ns : (s + 1) * ns] for s in range(rows)))
    leave(chunks - 1, sb)
    y = (y_s[...].reshape(delta.shape) + skip_ref[...] * act).astype(bf16)
    y_ref[...] = y
    gated_ref[...] = (y.astype(f32) * (z * sigmoid(z))).astype(bf16)


def forward_kernel(rows, layer_of, sizes, *refs):
    n = len(layer_of)
    rank, ns, taps, narrow, blocks = sizes
    (h_ref, gain_ref, wx_ref, wz_ref, full_n, half_n, mask_ref, half_w, kill_ref, full_w, full_ref), refs = refs[:11], refs[11:]
    cut = Packed(rank, ns, taps)
    kern_ref, off_ref, xp_ref = cut.kernel(full_n), cut.offset(full_n), cut.xproj(half_n)
    dtw_ref, bias_ref, rate_ref = cut.dtproj(half_w), cut.bias(full_w), cut.rate(full_w)
    skip_ref, rates_ref = cut.skip(full_w), cut.rate(full_ref)
    srcs, refs = refs[:n], refs[n:]
    (normed_ref, x_ref, z_ref, halo_ref, act_ref, rank_t_ref, bb_ref, cc_ref, delta_ref, sum_ref, y_ref, gated_ref,
     keep_ref), refs = refs[:13], refs[13:]
    dsts, refs = refs[:n], refs[n:]
    (proj_s, x_s, tail_s, halo_s, act_s, z_s, rank2_s, cd_s, eff_s, u_s, sa, sb, y_s, delta_s, end_s, start_s,
     sum_s), refs = refs[:17], refs[17:]
    exch, (send, recv, hsend, hrecv) = refs[:10], refs[10:]
    here = Place()
    block = pl.program_id(0)
    front = 2 * narrow
    nb, cb = x_s.shape[2], eff_s.shape[2]
    per = cb // nb

    def halo(j):
        return push(tail_s.at[j], halo_s.at[j], hsend, hrecv, j, here.ring(1))

    @pl.when(block == 0)
    def _():
        greet(here.partners() + [here.ring(1), here.ring(-1)])
        proj_s[...] = jnp.zeros_like(proj_s)
        h = h_ref[...]
        normed_ref[...] = (
            h * lax.rsqrt(jnp.mean(h * h, axis=1, keepdims=True) + norm_eps) * gain_ref[...]
        ).astype(bf16)

    jobs = [
        Gather(here, src.at[layer], dst, send, recv, GATHER_SEMS * i)
        for i, (src, dst, layer) in enumerate(zip(srcs, dsts, layer_of))
    ]
    plans = [FORWARD_ONE if src.shape[1] * 32 < h_ref.shape[1] * 4 else FORWARD_EARLY for src in srcs]
    for job, plan in zip(jobs, plans):
        beside(job, block, plan)

    @pl.when(block < narrow)
    def _():
        normed = normed_ref[...]
        x = dot_nt(normed, wx_ref[...])
        z = dot_nt(normed, wz_ref[...])
        z_ref[...] = z
        z_s[block // per, :, pl.ds(pl.multiple_of(lax.rem(block, per) * nb, nb), nb)] = z
        x16 = x.astype(bf16)
        x_ref[...] = x16
        x_s[block] = x16
        length = x.shape[0] // rows
        tail_s[block] = jnp.concatenate([x[(s + 1) * length - 8 : (s + 1) * length] for s in range(rows)], axis=0).astype(bf16)
        halo(block).start()

    @pl.when((block >= narrow) & (block < front))
    def _():
        j = block - narrow
        halo(j).wait()
        before = halo_s[j]
        halo_ref[...] = before
        act = conv_part(
            rows, x_s[j].astype(f32), before.astype(f32), kern_ref, off_ref, mask_ref, xp_ref, proj_s
        )
        act_ref[...] = act
        act_s[j // per, :, pl.ds(pl.multiple_of(lax.rem(j, per) * nb, nb), nb)] = act

    @pl.when(block == front - 1)
    def _():
        maps_part(rows, rank, ns, proj_s[...], rank2_s, rank_t_ref, bb_ref, cc_ref, cd_s)

    @pl.when((block >= front) & (block < front + blocks))
    def _():
        j = block - front
        delta, sums, ends = ends_part(
            rows, act_s[j], rank2_s, dtw_ref, bias_ref, kill_ref, rate_ref, bb_ref, eff_s, u_s
        )
        cols = pl.ds(pl.multiple_of(j * cb, cb), cb)
        delta_ref[...] = delta
        delta_s[j] = delta
        sum_s[:, cols] = sums
        end_s[:, cols] = ends

    @pl.when(block == front + blocks - 1)
    def _():
        sum_ref[...] = sum_s[...]
        exchange(here, False, rows, end_s, sum_s, rates_ref, start_s, exch)

    @pl.when(block >= front + blocks)
    def _():
        j = block - front - blocks
        cols = pl.ds(pl.multiple_of(j * cb, cb), cb)
        scan_part(rows, delta_s[j], act_s[j], z_s[j], kill_ref, rate_ref, skip_ref, bb_ref, cd_s,
                  start_s[:, cols], y_ref, gated_ref, keep_ref, eff_s, u_s, sa, sb, y_s)

    @pl.when(block == pl.num_programs(0) - 1)
    def _():
        for job, plan in reversed(list(zip(jobs, plans))):
            for phase in job.phases[len(plan) :]:
                phase()


def back_ends_part(rows, gg_ref, z_ref, y_ref, delta_ref, kill_ref, rate_ref, cc_ref, gz_ref, eff_s, gy_s):
    z = z_ref[...]
    gg = gg_ref[...]
    sig = sigmoid(z)
    gy = (gg * z * sig).astype(bf16)
    gz_ref[...] = (gg * y_ref[...].astype(f32) * sig * (1.0 + z * (1.0 - sig))).astype(bf16)
    cb = z.shape[1]
    eff_s[...] = chunked(delta_ref[...] + wide(kill_ref[...], cb))
    gy_s[...] = chunked(gy.astype(f32))
    rate = rate_ref[...] * LOG2E
    ns = rate.shape[0]
    length = z.shape[0] // rows
    chunks = length // STEPS
    inner = rows * STEPS * ns

    def chunk(i, flow):
        k = chunks - 1 - i
        flow = list(flow)
        for t in reversed(range(STEPS)):
            for s in range(rows):
                fade = jnp.exp2(rate * eff_s[s * chunks + k, t : t + 1, :])
                push = gy_s[s * chunks + k, t : t + 1, :] * tile_rows(cc_ref, k, (s * STEPS + t) * ns, ns, inner, cb)
                flow[s] = fade * (flow[s] + push)
        return tuple(flow)

    zero = jnp.zeros((ns, cb), f32)
    flow = lax.fori_loop(0, chunks, chunk, (zero,) * rows)
    return gy, jnp.concatenate(flow, axis=0)


def back_part(rows, act_ref, delta_ref, gy, kill_ref, rate_ref, skip_ref, dtw_ref, rank_t_ref, bb_ref, cc_ref, keep_ref,
              start, gact_ref, gdtw_ref, gbias_ref, grate_ref, gskip_ref,
              eff_s, u_s, gy_s, fade_s, held_s, sa, sb, gu_s, gd_s, gb_s, gc_s, grank_s):
    delta = delta_ref[...]
    act = act_ref[...]
    cb = delta.shape[1]
    eff_s[...] = chunked(delta + wide(kill_ref[...], cb))
    u_s[...] = chunked(delta * act)
    gy_s[...] = chunked(gy)
    rate_n = rate_ref[...]
    rate = rate_n * LOG2E
    ns = rate.shape[0]
    length = delta.shape[0] // rows
    chunks = length // STEPS
    pairs = rows * STEPS
    inner = pairs * ns
    half = ns // 2
    side = pairs * half
    pick = (
        lax.broadcasted_iota(jnp.int32, (2 * pairs, 2 * side), 0)
        == lax.broadcasted_iota(jnp.int32, (2 * pairs, 2 * side), 1) // half
    ).astype(bf16)

    def scan(k, carry, sums):
        flow, total = list(carry[0]), carry[1]
        state = [keep_ref[k, s * ns : (s + 1) * ns, :] for s in range(rows)]
        base = pl.multiple_of(k * inner, inner)
        for t in range(STEPS):
            for s in range(rows):
                at = (s * STEPS + t) * ns
                fade = jnp.exp2(rate * eff_s[s * chunks + k, t : t + 1, :])
                held = fade * state[s]
                fade_s[at : at + ns, :] = fade
                held_s[at : at + ns, :] = held
                drive = u_s[s * chunks + k, t : t + 1, :] * tile_rows(bb_ref, k, at, ns, inner, cb)
                state[s] = held + drive
                gc_s[pl.ds(base + at, ns), :] += lane_sum(state[s] * gy_s[s * chunks + k, t : t + 1, :])
        for t in reversed(range(STEPS)):
            for s in range(rows):
                at = (s * STEPS + t) * ns
                push = gy_s[s * chunks + k, t : t + 1, :] * tile_rows(cc_ref, k, at, ns, inner, cb)
                grad = flow[s] + push
                gb_s[pl.ds(base + at, ns), :] += lane_sum(grad * u_s[s * chunks + k, t : t + 1, :])
                w = grad * held_s[at : at + ns, :]
                total = total + w * eff_s[s * chunks + k, t : t + 1, :]
                gu = grad * tile_rows(bb_ref, k, at, ns, inner, cb)
                wa = w * rate_n
                low = (s * STEPS + t) * half
                sums[low : low + half, :] = gu[:half] + gu[half:]
                sums[side + low : side + low + half, :] = wa[:half] + wa[half:]
                flow[s] = fade_s[at : at + ns, :] * grad
        return tuple(flow), total

    def leave(k, sums):
        out = dot(pick, sums[...].astype(bf16))
        for s in range(rows):
            gu_s[s * chunks + k] = out[s * STEPS : (s + 1) * STEPS]
            gd_s[s * chunks + k] = out[pairs + s * STEPS : pairs + (s + 1) * STEPS]

    sb[...] = jnp.zeros_like(sb)

    def two(i, carry):
        k = chunks - 1 - 2 * i
        leave(jnp.minimum(k + 1, chunks - 1), sb)
        carry = scan(k, carry, sa)
        leave(k, sa)
        return scan(k - 1, carry, sb)

    first = tuple(start[s * ns : (s + 1) * ns] for s in range(rows))
    _, total = lax.fori_loop(0, chunks // 2, two, (first, jnp.zeros((ns, cb), f32)))
    leave(0, sb)
    grate_ref[...] = total * rate_n
    gu = gu_s[...].reshape(delta.shape)
    gact_ref[...] = gu * delta + skip_ref[...] * gy
    gskip_ref[...] = jnp.sum(gy * act, axis=0, keepdims=True)
    gpre = (gu * act + gd_s[...].reshape(delta.shape)) * (1.0 - jnp.exp(-delta))
    gbias_ref[...] = jnp.sum(gpre, axis=0, keepdims=True)
    gpre16 = gpre.astype(bf16)
    gdtw_ref[...] = dot(rank_t_ref[...], gpre16)
    grank_s[...] += dot_nt(gpre16, dtw_ref[...])


def fold_part(rows, ns, gproj_ref, gproj_t_ref, gb_s, gc_s, grank_s):
    pairs = rows * STEPS
    inner = pairs * ns
    chunks = gb_s.shape[0] // inner
    ones = jnp.ones((128, 128), bf16)
    lane = lax.broadcasted_iota(jnp.int32, (pairs, ns, 128), 2)
    spot = lax.broadcasted_iota(jnp.int32, (pairs, ns, 128), 1)
    rank = grank_s.shape[1]

    def fold(ref, k):
        high, low = halves(ref[k * inner : (k + 1) * inner, :])
        v = (dot(high, ones) + dot(low, ones)).reshape(pairs, ns, 128)
        return jnp.sum(jnp.where(lane == spot, v, 0.0), axis=1)[:, :ns]

    for k in range(chunks):
        gb, gc = fold(gb_s, k), fold(gc_s, k)
        for s in range(rows):
            here = slice((s * chunks + k) * STEPS, (s * chunks + k + 1) * STEPS)
            mine = slice(s * STEPS, (s + 1) * STEPS)
            gproj_ref[here, :] = jnp.concatenate([grank_s[here, :], gb[mine], gc[mine]], axis=1)
    gproj_t_ref[...] = gproj_ref[...].T


def backward_kernel(rows, n, sizes, *refs):
    blocks, narrow, rank, ns, taps = sizes
    (gg_ref, z_ref, y_ref, wdelta_ref, full_w, kill_ref, full_ref, sum_ref, act_ref, delta_ref, full_n,
     half_n, rank_t_ref, bb_ref, cc_ref, keep_ref, x_ref, halo_ref, mask_ref) = refs[:19]
    refs = refs[19:]
    cut = Packed(rank, ns, taps)
    wrate_ref, rates_ref, rate_ref, skip_ref = cut.rate(full_w), cut.rate(full_ref), cut.rate(full_n), cut.skip(full_n)
    dtw_ref, xp_ref, kern_ref, off_ref = cut.dtproj(half_n), cut.xproj(half_n), cut.kernel(full_n), cut.offset(full_n)
    srcs, refs = refs[:n], refs[n:]
    (mixed_ref, packed_ref), refs = refs[:2], refs[2:]
    sums, refs = refs[:n], refs[n:]
    (weff_s, wgy_s, gyall_s, end_s, start_s, gz_s, gact_s, gproj_s, gproj_t_s, gend_s, edge_s, late_s, gdtw_s, gbias_s, grate_s,
     gskip_s, gxp_s, gkern_s, goff_s), refs = refs[:19], refs[19:]
    (eff_s, u_s, gy_s, fade_s, held_s, sa, sb, gu_s, gd_s, gb_s, gc_s, grank_s), refs = refs[:12], refs[12:]
    exch, (esend, erecv), refs = refs[:10], refs[10:12], refs[12:]
    here = Place()
    block = pl.program_id(0)
    wide_cb, cb = gg_ref.shape[1], act_ref.shape[1]
    c = wide_cb * blocks

    def edge(j):
        return push(edge_s.at[j], late_s.at[j], esend, erecv, j, here.ring(-1))

    @pl.when(block == 0)
    def _():
        greet(here.partners() + [here.ring(1), here.ring(-1)])
        gc_s[...] = jnp.zeros_like(gc_s)
        gb_s[...] = jnp.zeros_like(gb_s)
        grank_s[...] = jnp.zeros_like(grank_s)

    beside(Reduces(srcs, sums, refs), block, BACKWARD_STEPS)

    @pl.when(block < blocks)
    def _():
        gy, flow = back_ends_part(
            rows, gg_ref, z_ref, y_ref, wdelta_ref, kill_ref, wrate_ref, cc_ref, gz_s, weff_s, wgy_s
        )
        cols = pl.ds(pl.multiple_of(block * wide_cb, wide_cb), wide_cb)
        mixed_ref[:, pl.ds(pl.multiple_of(c + block * wide_cb, wide_cb), wide_cb)] = gz_s[...]
        gyall_s[:, cols] = gy.astype(f32)
        end_s[:, cols] = flow

    @pl.when(block == blocks - 1)
    def _():
        exchange(here, True, rows, end_s, sum_ref, rates_ref, start_s, exch)

    @pl.when((block >= blocks) & (block < blocks + narrow))
    def _():
        j = block - blocks
        cols = pl.ds(pl.multiple_of(j * cb, cb), cb)
        back_part(rows, act_ref, delta_ref, gyall_s[:, cols], kill_ref, rate_ref, skip_ref, dtw_ref, rank_t_ref,
                  bb_ref, cc_ref, keep_ref, start_s[:, cols], gact_s.at[j], gdtw_s.at[j], gbias_s.at[j], grate_s.at[j], gskip_s.at[j],
                  eff_s, u_s, gy_s, fade_s, held_s, sa, sb, gu_s, gd_s, gb_s, gc_s, grank_s)

    @pl.when(block == blocks + narrow - 1)
    def _():
        fold_part(rows, rate_ref.shape[0], gproj_s, gproj_t_s, gb_s, gc_s, grank_s)

    @pl.when(block >= blocks + narrow)
    def _():
        j = block - blocks - narrow
        cols = pl.ds(pl.multiple_of(j * cb, cb), cb)
        gx, edges = conv_back_part(
            rows, x_ref, halo_ref, kern_ref, off_ref, mask_ref, act_ref, gact_s[j], gproj_s, gproj_t_s, xp_ref,
            gxp_s, gkern_s, goff_s
        )
        rows_of = [gxp_s[...], gdtw_s[j], grate_s[j], gkern_s[...], goff_s[...], gbias_s[j], gskip_s[j]]
        count = sum(v.shape[0] for v in rows_of)
        rows_of.append(jnp.zeros((packed_ref.shape[0] - count, cb), f32))
        packed_ref[...] = jnp.concatenate(rows_of, axis=0).astype(bf16)
        edge_s[j] = edges.astype(bf16)
        edge(j).start()
        mixed_ref[:, cols] = gx.astype(bf16)
        length = gx.shape[0] // rows
        gend_s[j] = jnp.concatenate([gx[(s + 1) * length - 16 : (s + 1) * length] for s in range(rows)], axis=0)

    @pl.when(block == pl.num_programs(0) - 1)
    def _():
        more = jnp.where((here.z == 3) & (here.c == 1), 0.0, 1.0)
        length = mixed_ref.shape[0] // rows
        for j in range(narrow):
            edge(j).wait()
            late = late_s[j].astype(f32) * more
            for s in range(rows):
                end = gend_s[j, 16 * s : 16 * s + 16]
                fixed = jnp.concatenate([end[:8], end[8:] + late[8 * s : 8 * s + 8]], axis=0)
                mixed_ref[(s + 1) * length - 16 : (s + 1) * length, j * cb : (j + 1) * cb] = fixed.astype(bf16)
        Reduces(srcs, sums, refs).run(-1)


def ends_kernel(rows, act_ref, rank2_ref, dtw_ref, bias_ref, kill_ref, rate_ref, bb_ref,
                delta_ref, end_ref, sum_ref, eff_s, u_s):
    delta_ref[...], sum_ref[...], end_ref[...] = ends_part(
        rows, act_ref[...], rank2_ref, dtw_ref, bias_ref, kill_ref, rate_ref, bb_ref, eff_s, u_s
    )


def scan_kernel(rows, act_ref, delta_ref, z_ref, kill_ref, rate_ref, skip_ref, bb_ref, cd_ref, start_ref, *refs):
    scan_part(rows, delta_ref[...], act_ref[...], z_ref[...], kill_ref, rate_ref, skip_ref, bb_ref, cd_ref, start_ref[...], *refs)


def back_ends_kernel(rows, gg_ref, z_ref, y_ref, delta_ref, kill_ref, rate_ref, cc_ref,
                     gy_ref, gz_ref, end_ref, eff_s, gy_s):
    gy_ref[...], end_ref[...] = back_ends_part(
        rows, gg_ref, z_ref, y_ref, delta_ref, kill_ref, rate_ref, cc_ref, gz_ref, eff_s, gy_s
    )


def back_kernel(rows, act_ref, delta_ref, gy_ref, kill_ref, rate_ref, skip_ref, dtw_ref, rank_t_ref,
                bb_ref, cc_ref, keep_ref, start_ref,
                gact_ref, gproj_ref, gproj_t_ref, gdtw_ref, gbias_ref, grate_ref, gskip_ref, *scratch):
    gb_s, gc_s, grank_s = scratch[-3:]

    @pl.when(pl.program_id(0) == 0)
    def _():
        gc_s[...] = jnp.zeros_like(gc_s)
        gb_s[...] = jnp.zeros_like(gb_s)
        grank_s[...] = jnp.zeros_like(grank_s)

    back_part(rows, act_ref, delta_ref, gy_ref[...].astype(f32), kill_ref, rate_ref, skip_ref, dtw_ref, rank_t_ref,
              bb_ref, cc_ref, keep_ref, start_ref[...], gact_ref, gdtw_ref, gbias_ref, grate_ref, gskip_ref, *scratch)

    @pl.when(pl.program_id(0) == pl.num_programs(0) - 1)
    def _():
        fold_part(rows, rate_ref.shape[0], gproj_ref, gproj_t_ref, gb_s, gc_s, grank_s)


def conv_back_part(rows, x_ref, halo_ref, kern_ref, off_ref, mask_ref, act_ref, gact, gproj_ref,
                   gproj_t_ref, xp_ref, gxp_ref, gkern_ref, goff_ref):
    x = x_ref[...].astype(bf16).astype(f32)
    cb = x.shape[1]
    halo = halo_ref[...].astype(f32)
    kernel = kern_ref[...]
    taps = kernel.shape[0]
    masks = [wide(mask_ref[i], cb) for i in range(taps - 1)]
    pre = conv_sum(x, halo, kernel, off_ref[...], masks, rows)
    sig = sigmoid(pre)
    act16 = act_ref[...].astype(bf16)
    gxp_ref[...] = dot(gproj_t_ref[...].astype(bf16), act16)
    g_act = gact + dot(gproj_ref[...].astype(bf16), xp_ref[...])
    gpre = g_act * sig * (1.0 + pre * (1.0 - sig))
    goff_ref[...] = jnp.sum(gpre, axis=0, keepdims=True)
    length = x.shape[0] // rows
    place = lax.broadcasted_iota(jnp.int32, (length, cb), 0)
    gk = [jnp.zeros((1, cb), f32) for _ in range(taps)]
    gxs, edges = [], []
    for s in range(rows):
        here = slice(s * length, (s + 1) * length)
        g = gpre[here]
        ext = jnp.concatenate([halo[8 * s : 8 * s + 8], x[here]], axis=0)
        gk[taps - 1] = gk[taps - 1] + jnp.sum(g * x[here], axis=0, keepdims=True)
        gx = kernel[taps - 1 : taps] * g
        edge = jnp.zeros((length, cb), f32)
        for lag in range(1, taps):
            gm = g * masks[lag - 1][here]
            moved = pltpu.roll(ext, lag, 0)[8:]
            j = taps - 1 - lag
            gk[j] = gk[j] + jnp.sum(gm * moved, axis=0, keepdims=True)
            up = pltpu.roll(kernel[j : j + 1] * gm, length - lag, 0)
            inside = place < length - lag
            gx = gx + jnp.where(inside, up, 0.0)
            edge = edge + jnp.where(inside, 0.0, up)
        gxs.append(gx)
        edges.append(edge[length - 8 :])
    gkern_ref[...] = jnp.concatenate(gk, axis=0)
    return jnp.concatenate(gxs, axis=0), jnp.concatenate(edges, axis=0)


def conv_back_kernel(rows, x_ref, halo_ref, kern_ref, off_ref, mask_ref, act_ref, gact_ref, gproj_ref,
                     gproj_t_ref, xp_ref, gx_ref, edge_ref, *outs):
    gx_ref[...], edge_ref[...] = conv_back_part(
        rows, x_ref, halo_ref, kern_ref, off_ref, mask_ref, act_ref, gact_ref[...], gproj_ref, gproj_t_ref, xp_ref, *outs
    )


def col(rows, cb, shift=0):
    return pl.BlockSpec((rows, cb), lambda j: (0, j + shift))


def whole(*shape):
    return pl.BlockSpec(shape, lambda j: (0,) * len(shape))


def call(body, blocks, ins, outs, scratch, args, ident=None):
    more = {} if ident is None else dict(collective_id=ident, has_side_effects=True)
    return pl.pallas_call(
        body,
        grid=(blocks,),
        in_specs=ins,
        out_specs=[spec for spec, _, _ in outs],
        out_shape=[jax.ShapeDtypeStruct(shape, kind) for _, shape, kind in outs],
        scratch_shapes=scratch,
        compiler_params=pltpu.CompilerParams(
            dimension_semantics=("arbitrary",), vmem_limit_bytes=VMEM, **more
        ),
    )(*args)


class Mixer:
    def __init__(self, layers, rows, length, channels, ns, rank, taps):
        self.layers = layers
        self.rows, self.length, self.c, self.ns, self.rank, self.taps = rows, length, channels, ns, rank, taps
        self.tokens = rows * length
        self.chunks = length // STEPS
        self.pairs = rows * STEPS
        self.inner = self.pairs * ns
        self.width = rank + 2 * ns

    def conv(self, projected, halo, p, masks):
        t, c, cb = self.tokens, self.c, CB
        tall = (t * self.ns, 128)
        out = call(
            functools.partial(conv_kernel, self.rows, (self.rank, self.ns)), c // cb,
            [col(t, cb), col(8 * self.rows, cb), col(self.taps, cb), col(1, cb), whole(*masks.shape), col(self.width, cb)],
            [(col(t, cb), (t, c), f32), (whole(t, 2 * self.rank), (t, 2 * self.rank), bf16),
             (whole(self.rank, t), (self.rank, t), bf16), (whole(*tall), tall, f32), (whole(*tall), tall, f32),
             (whole(t, self.inner), (t, self.inner), f32)],
            [pltpu.VMEM((t, self.width), f32)], (projected, halo, p["conv_w"], p["conv_b"], masks, p["xproj"]),
        )
        m = dict(zip(("rank2", "rank_t", "bb", "cc", "cd"), out[1:]))
        m["cd"] = m["cd"].reshape(-1, STEPS, self.inner)
        return out[0], m

    def scratch3(self, cb):
        return pltpu.VMEM((self.tokens // STEPS, STEPS, cb), f32)

    def wide_scratch(self, kind, cb):
        return pltpu.VMEM((self.inner, cb), kind)

    def forward(self, i, h, gain, in_full, half, full, masks, kill, gathers, ident):
        t, c, sn, cb, nb, ns, d = self.tokens, self.c, self.rows * self.ns, CB_SCAN, CB, self.ns, h.shape[1]
        narrow, blocks = c // nb, c // cb
        front = 2 * narrow
        hn, fn = half.shape[0] // self.layers, full.shape[0] // self.layers

        def first(rows):
            return pl.BlockSpec((rows, nb), lambda j: (0, jnp.minimum(j, narrow - 1)))

        def second(rows):
            return pl.BlockSpec((rows, nb), lambda j: (0, jnp.clip(j - narrow, 0, narrow - 1)))

        def early(rows):
            return pl.BlockSpec((rows, cb), lambda j: (0, jnp.clip(j - front, 0, blocks - 1)))

        def both(rows):
            return pl.BlockSpec((rows, cb), lambda j: (0, lax.rem(jnp.maximum(j - front, 0), blocks)))

        def late(rows):
            return pl.BlockSpec((rows, cb), lambda j: (0, jnp.maximum(j - front - blocks, 0)))

        def at(spec):
            return pl.BlockSpec(spec.block_shape, lambda j: (i, spec.index_map(j)[1]))

        wx = pl.BlockSpec((nb, d), lambda j: (jnp.minimum(j, narrow - 1), 0))
        wz = pl.BlockSpec((nb, d), lambda j: (jnp.minimum(j, narrow - 1) + narrow, 0))
        n = len(gathers)
        keep = pl.BlockSpec((self.chunks, sn, cb), lambda j: (0, 0, jnp.maximum(j - front - blocks, 0)))
        sems = [pltpu.SemaphoreType.DMA((GATHER_SEMS * max(n, 1),))] * 2 + [pltpu.SemaphoreType.DMA((narrow,))] * 2
        tall = (t * ns, 128)
        hr = 8 * self.rows
        out = call(
            functools.partial(forward_kernel, self.rows, [k for _, k in gathers], (self.rank, ns, self.taps, narrow, blocks)), front + 2 * blocks,
            [whole(t, d), whole(1, d), wx, wz, at(second(fn)), at(second(hn)), whole(*masks.shape), at(early(hn)),
             whole(*kill.shape), at(both(fn)), pl.BlockSpec((fn, c), lambda j: (i, 0))] + [ANY] * n,
            [(whole(t, d), (t, d), bf16), (first(t), (t, c), bf16), (first(t), (t, c), f32), (second(hr), (hr, c), bf16),
             (second(t), (t, c), f32), (whole(self.rank, t), (self.rank, t), bf16), (whole(*tall), tall, f32),
             (whole(*tall), tall, f32), (early(t), (t, c), f32), (whole(self.rows, c), (self.rows, c), f32),
             (late(t), (t, c), bf16), (late(t), (t, c), bf16), (keep, (self.chunks, sn, c), f32)]
            + [(ANY, (2, 2, 4, 2) + g.shape[1:], g.dtype) for g, _ in gathers],
            [pltpu.VMEM((t, self.width), f32), pltpu.VMEM((narrow, t, nb), bf16), pltpu.VMEM((narrow, hr, nb), bf16),
             pltpu.VMEM((narrow, hr, nb), bf16), pltpu.VMEM((blocks, t, cb), f32), pltpu.VMEM((blocks, t, cb), f32),
             pltpu.VMEM((t, 2 * self.rank), bf16), pltpu.VMEM((t // STEPS, STEPS, self.inner), f32),
             self.scratch3(cb), self.scratch3(cb), self.wide_scratch(bf16, cb), self.wide_scratch(bf16, cb),
             self.scratch3(cb), pltpu.VMEM((blocks, t, cb), f32), pltpu.VMEM((sn, c), f32), pltpu.VMEM((sn, c), f32),
             pltpu.VMEM((self.rows, c), f32)] + exchange_scratch(self.rows, sn, c) + sems,
            (h, gain, in_full, in_full, full, half, masks, half, kill, full, full, *[g for g, _ in gathers]),
            ident,
        )
        return out[:13], [g.reshape(-1, g.shape[-1]) for g in out[13:]]

    def backward(self, i, gg, x, z, halo, y, act, delta, total, m, half, full, masks, kill, keep, sums, ident):
        t, c, sn, ns, cb, wcb = self.tokens, self.c, self.rows * self.ns, self.ns, CB_BACK, CB_ENDS
        blocks, narrow = c // wcb, c // cb

        def early(rows):
            return pl.BlockSpec((rows, wcb), lambda j: (0, jnp.minimum(j, blocks - 1)))

        def late(rows):
            return pl.BlockSpec((rows, cb), lambda j: (0, jnp.clip(j - blocks, 0, narrow - 1)))

        def last(rows):
            return pl.BlockSpec((rows, cb), lambda j: (0, jnp.maximum(j - blocks - narrow, 0)))

        def twice(rows):
            return pl.BlockSpec((rows, cb), lambda j: (0, lax.rem(jnp.maximum(j - blocks, 0), narrow)))

        def at(spec):
            return pl.BlockSpec(spec.block_shape, lambda j: (i, spec.index_map(j)[1]))

        hn, fn = half.shape[0] // self.layers, full.shape[0] // self.layers
        kept = pl.BlockSpec((self.chunks, sn, cb), lambda j: (0, 0, jnp.clip(j - blocks, 0, narrow - 1)))
        tall = m["bb"].shape
        hr = 8 * self.rows
        pack = self.width + self.rank + ns + self.taps + 3
        pack += -pack % 64
        more_in, more_out, more_scratch = reduce_parts(sums)
        sems = [pltpu.SemaphoreType.DMA((narrow,))] * 2
        out = call(
            functools.partial(backward_kernel, self.rows, len(sums), (blocks, narrow, self.rank, ns, self.taps)), blocks + 2 * narrow,
            [early(t), early(t), early(t), early(t), at(early(fn)), whole(*kill.shape), pl.BlockSpec((fn, c), lambda j: (i, 0)),
             whole(self.rows, c), twice(t), late(t), at(twice(fn)), at(twice(hn)), whole(*m["rank_t"].shape), whole(*tall),
             whole(*tall), kept, last(t), last(hr), whole(*masks.shape)] + [ANY] * len(sums),
            [(whole(t, 2 * c), (t, 2 * c), bf16), (last(pack), (pack, c), bf16)]
            + [(whole(*v.shape), v.shape, f32) for v in more_out],
            [self.scratch3(wcb)] * 2 + [pltpu.VMEM((t, c), f32), pltpu.VMEM((sn, c), f32), pltpu.VMEM((sn, c), f32)]
            + [pltpu.VMEM((t, wcb), bf16), pltpu.VMEM((narrow, t, cb), f32), pltpu.VMEM((t, self.width), f32),
               pltpu.VMEM((self.width, t), f32), pltpu.VMEM((narrow, 2 * hr, cb), f32), pltpu.VMEM((narrow, hr, cb), bf16),
               pltpu.VMEM((narrow, hr, cb), bf16)]
            + [pltpu.VMEM((narrow, k, cb), f32) for k in (self.rank, 1, ns, 1)]
            + [pltpu.VMEM((k, cb), f32) for k in (self.width, self.taps, 1)]
            + [self.scratch3(cb)] * 3 + [self.wide_scratch(f32, cb)] * 4 + [self.scratch3(cb)] * 2
            + [pltpu.VMEM(tall, f32)] * 2 + [pltpu.VMEM((t, self.rank), f32)] + exchange_scratch(self.rows, sn, c)
            + sems + more_scratch,
            (gg, z, y, delta, full, kill, full, total, act, delta, full, half, m["rank_t"], m["bb"], m["cc"], keep, x, halo,
             masks, *more_in),
            ident,
        )
        return out[:2], out[2:]

    def ends(self, act, m, p, kill):
        t, c, sn, cb = self.tokens, self.c, self.rows * self.ns, CB_ENDS
        return call(
            functools.partial(ends_kernel, self.rows), c // cb,
            [col(t, cb), whole(*m["rank2"].shape), col(self.rank, cb), col(1, cb), whole(*kill.shape), col(self.ns, cb),
             whole(*m["bb"].shape)],
            [(col(t, cb), (t, c), f32), (col(sn, cb), (sn, c), f32), (col(self.rows, cb), (self.rows, c), f32)],
            [self.scratch3(cb), self.scratch3(cb)],
            (act, m["rank2"], p["dtproj"], p["dt_b"], kill, p["rate"], m["bb"]),
        )

    def scan(self, act, delta, projected, m, p, kill, start):
        t, c, sn, cb = self.tokens, self.c, self.rows * self.ns, CB_SCAN
        keep = pl.BlockSpec((self.chunks, sn, cb), lambda j: (0, 0, j))
        return call(
            functools.partial(scan_kernel, self.rows), c // cb,
            [col(t, cb), col(t, cb), col(t, cb, c // cb), whole(*kill.shape), col(self.ns, cb), col(1, cb),
             whole(*m["bb"].shape), whole(*m["cd"].shape), col(sn, cb)],
            [(col(t, cb), (t, c), bf16), (col(t, cb), (t, c), bf16), (keep, (self.chunks, sn, c), f32)],
            [self.scratch3(cb), self.scratch3(cb), self.wide_scratch(bf16, cb), self.wide_scratch(bf16, cb),
             self.scratch3(cb)],
            (act, delta, projected, kill, p["rate"], p["skip"], m["bb"], m["cd"], start),
        )

    def back_ends(self, gg, projected, y, delta, m, p, kill):
        t, c, sn, cb = self.tokens, self.c, self.rows * self.ns, CB_ENDS
        return call(
            functools.partial(back_ends_kernel, self.rows), c // cb,
            [col(t, cb), col(t, cb, c // cb), col(t, cb), col(t, cb), whole(*kill.shape), col(self.ns, cb),
             whole(*m["cc"].shape)],
            [(col(t, cb), (t, c), bf16), (col(t, cb), (t, c), bf16), (col(sn, cb), (sn, c), f32)],
            [self.scratch3(cb), self.scratch3(cb)],
            (gg, projected, y, delta, kill, p["rate"], m["cc"]),
        )

    def back(self, act, delta, gy, m, p, kill, keep, start):
        t, c, sn, ns, cb = self.tokens, self.c, self.rows * self.ns, self.ns, CB_BACK
        kept = pl.BlockSpec((self.chunks, sn, cb), lambda j: (0, 0, j))
        tall = m["bb"].shape
        return call(
            functools.partial(back_kernel, self.rows), c // cb,
            [col(t, cb), col(t, cb), col(t, cb), whole(*kill.shape), col(ns, cb), col(1, cb), col(self.rank, cb),
             whole(*m["rank_t"].shape), whole(*tall), whole(*tall), kept, col(sn, cb)],
            [(col(t, cb), (t, c), f32), (whole(t, self.width), (t, self.width), f32),
             (whole(self.width, t), (self.width, t), f32), (col(self.rank, cb), (self.rank, c), f32),
             (col(1, cb), (1, c), f32), (col(ns, cb), (ns, c), f32), (col(1, cb), (1, c), f32)],
            [self.scratch3(cb)] * 3 + [self.wide_scratch(f32, cb)] * 4 + [self.scratch3(cb)] * 2
            + [pltpu.VMEM(tall, f32)] * 2 + [pltpu.VMEM((t, self.rank), f32)],
            (act, delta, gy, kill, p["rate"], p["skip"], p["dtproj"], m["rank_t"], m["bb"], m["cc"], keep, start),
        )

    def conv_back(self, projected, halo, p, masks, act, gact, gproj, gproj_t):
        t, c, cb = self.tokens, self.c, CB
        return call(
            functools.partial(conv_back_kernel, self.rows), c // cb,
            [col(t, cb), col(8 * self.rows, cb), col(self.taps, cb), col(1, cb), whole(*masks.shape), col(t, cb),
             col(t, cb), whole(t, self.width), whole(self.width, t), col(self.width, cb)],
            [(col(t, cb), (t, c), f32), (col(8 * self.rows, cb), (8 * self.rows, c), f32),
             (col(self.width, cb), (self.width, c), f32), (col(self.taps, cb), (self.taps, c), f32),
             (col(1, cb), (1, c), f32)],
            [], (projected, halo, p["conv_w"], p["conv_b"], masks, act, gact, gproj, gproj_t, p["xproj"]),
        )


MESH = pl.DeviceIdType.MESH
ANY = pl.BlockSpec(memory_space=pl.ANY)
INV = pl.BlockSpec(memory_space=pltpu.VMEM)


class Place:
    def __init__(self):
        r, b = lax.axis_index("rows"), lax.axis_index("bytes")
        self.y, self.x, self.z, self.c = r // 2, lax.rem(r, 2), b // 2, lax.rem(b, 2)

    def at(self, y=None, x=None, z=None, c=None):
        y = self.y if y is None else y
        x = self.x if x is None else x
        z = self.z if z is None else z
        c = self.c if c is None else c
        return (y * 2 + x, z * 2 + c)

    def over(self, k):
        return lax.rem(self.z + k, 4)

    def ring(self, step):
        b = lax.rem(self.z * 2 + self.c + 8 + step, 8)
        return self.at(z=b // 2, c=lax.rem(b, 2))

    def partners(self):
        return [self.at(c=1 - self.c), self.at(x=1 - self.x), self.at(y=1 - self.y)] + [
            self.at(z=self.over(k)) for k in (1, 2, 3)
        ]


def greet(partners):
    barrier = pltpu.get_barrier_semaphore()
    for p in partners:
        pl.semaphore_signal(barrier, inc=1, device_id=p, device_id_type=MESH)
    pl.semaphore_wait(barrier, len(partners))


def push(src, dst, send, recv, i, device):
    return pltpu.make_async_remote_copy(
        src_ref=src, dst_ref=dst, send_sem=send.at[i], recv_sem=recv.at[i], device_id=device, device_id_type=MESH
    )


GATHER_SEMS = 36
TURN = (1, 3, 2)


class Gather:
    def __init__(self, here, src, dst, send, recv, base):
        self.here, self.src, self.dst, self.send, self.recv, self.base = here, src, dst, send, recv, base
        self.h = src.shape[0] // 2
        part = functools.partial
        self.phases = [self.begin, part(self.side, 0), part(self.come, 1), part(self.come, 3), part(self.side, 1),
                       part(self.come, 2), part(self.side, 3), part(self.side, 2), self.cross, self.last]

    def source(self, k):
        return lax.rem(self.here.z + 4 - k, 4)

    def own(self):
        h = self.here
        return pltpu.make_async_copy(self.src, self.dst.at[h.y, h.x, h.z, h.c], self.send.at[self.base + 35])

    def push(self, src, dst, i, device):
        return push(src, dst, self.send, self.recv, self.base + i, device)

    def line(self, k):
        h = self.here
        return self.push(self.src, self.dst.at[h.y, h.x, h.z, h.c], k - 1, h.at(z=h.over(k)))

    def sides(self, k):
        h = self.here
        dst = self.dst.at[h.y, h.x, self.source(k), h.c]
        src = self.src if k == 0 else dst
        return [
            self.push(src, dst, 3 + k, h.at(x=1 - h.x)),
            self.push(src, dst, 7 + k, h.at(y=1 - h.y)),
        ]

    def across(self, k):
        h, z = self.here, self.source(k)
        top, low = pl.ds(0, self.h), pl.ds(self.h, self.h)
        u, v = self.dst.at[1 - h.y, h.x, z, h.c, top], self.dst.at[h.y, 1 - h.x, z, h.c, low]
        return [
            self.push(u, u, 11 + k, h.at(x=1 - h.x)),
            self.push(v, v, 15 + k, h.at(y=1 - h.y)),
        ]

    def core(self, k, part):
        h, z = self.here, self.source(k)
        y, x = ((h.y, h.x), (h.y, 1 - h.x), (1 - h.y, h.x), (1 - h.y, 1 - h.x))[part]
        dst = self.dst.at[y, x, z, h.c]
        src = self.src if (k == 0 and part == 0) else dst
        return self.push(src, dst, 19 + 4 * k + part, h.at(c=1 - h.c))

    def begin(self):
        self.own().start()
        for k in TURN:
            self.line(k).start()
        for copy in self.sides(0):
            copy.start()
        self.core(0, 0).start()

    def come(self, k):
        self.line(k).wait_recv()
        for copy in self.sides(k):
            copy.start()
        self.core(k, 0).start()

    def side(self, k):
        for copy in self.sides(k):
            copy.wait_recv()
        for copy in self.across(k):
            copy.start()
        self.core(k, 1).start()
        self.core(k, 2).start()

    def cross(self):
        for k in (0,) + TURN:
            for copy in self.across(k):
                copy.wait_recv()
            self.core(k, 3).start()

    def last(self):
        self.own().wait()
        for k in TURN:
            self.line(k).wait_send()
        for k in range(4):
            for copy in self.sides(k) + self.across(k):
                copy.wait_send()
            for part in range(4):
                self.core(k, part).wait()


class GatherBytes:
    def __init__(self, here, src, dst, send, recv, base):
        self.here, self.src, self.dst, self.send, self.recv, self.base = here, src, dst, send, recv, base
        self.w = src.shape[1]
        self.q = src.shape[0] // 4
        self.phases = [self.begin, self.second, self.third, self.fourth, self.last]

    def spot(self, z, c, q=None, n=1):
        cols = pl.ds(pl.multiple_of((z * 2 + c) * self.w, self.w), self.w)
        if q is None:
            return self.dst.at[:, cols]
        return self.dst.at[pl.ds(pl.multiple_of(q * self.q, self.q), n * self.q), cols]

    def source(self, k):
        return lax.rem(self.here.z + 4 - k, 4)

    def push(self, src, dst, i, device):
        return push(src, dst, self.send, self.recv, self.base + i, device)

    def own(self):
        h = self.here
        return pltpu.make_async_copy(self.src, self.spot(h.z, h.c), self.send.at[self.base + 13])

    def line(self, k):
        h = self.here
        q = h.y * 2 + h.x
        src = self.src.at[pl.ds(pl.multiple_of(q * self.q, self.q), self.q)]
        return self.push(src, self.spot(h.z, h.c, q), k - 1, h.at(z=h.over(k)))

    def over_x(self, k):
        h = self.here
        u = self.spot(self.source(k), h.c, h.y * 2 + h.x)
        return self.push(u, u, 2 + k, h.at(x=1 - h.x))

    def over_y(self, k):
        h = self.here
        u = self.spot(self.source(k), h.c, h.y * 2, 2)
        return self.push(u, u, 5 + k, h.at(y=1 - h.y))

    def core(self, k):
        h = self.here
        u = self.spot(self.source(k), h.c)
        src = self.src if k == 0 else u
        return self.push(src, u, 9 + k, h.at(c=1 - h.c))

    def begin(self):
        self.own().start()
        for k in TURN:
            self.line(k).start()
        self.core(0).start()

    def second(self):
        for k in TURN:
            self.line(k).wait_recv()
            self.over_x(k).start()

    def third(self):
        for k in TURN:
            self.over_x(k).wait_recv()
            self.over_y(k).start()

    def fourth(self):
        for k in TURN:
            self.over_y(k).wait_recv()
            self.core(k).start()

    def last(self):
        self.own().wait()
        for k in TURN:
            self.line(k).wait_send()
            self.over_x(k).wait_send()
            self.over_y(k).wait_send()
        for k in range(4):
            self.core(k).wait()


def run_phases(jobs, plans):
    for step in range(max(plan[-1] for plan in plans) + 1):
        for job, plan in zip(jobs, plans):
            for phase, at in zip(job.phases, plan):
                if at == step:
                    phase()


GATHER_PLAN = (0, 2, 4, 6, 8, 10, 12, 14, 16, 18)
NEXT_PLAN = (0, 3, 7, 9, 11, 13, 15, 17, 19, 20)
SMALL_PLAN = (0, 3, 6, 9, 15)
REDUCE_PLAN = (0, 1, 2, 3, 4, 5, 6, 7, 8, 9, 10, 11)
SIDES_PLAN = (8, 10)
ALL_PLAN = (6, 8, 9, 10, 11)
SMALL_REDUCE = (0, 1, 2, 2, 2, 2, 2, 5, 5, 5, 5, 7)


def gather_kernel(xp_ref, dtw_ref, rate_ref, kern_ref, off_ref, bias_ref, skip_ref, in_ref, out_ref,
                  half_ref, full_ref, win_ref, wout_ref, half_s, full_s, send, recv):
    here = Place()
    greet(here.partners())
    layers = xp_ref.shape[0]
    hn, fn = half_s.shape[0] // layers, full_s.shape[0] // layers
    for i in range(layers):
        wt = xp_ref[i].astype(f32).T.astype(bf16)
        half_s[i * hn : i * hn + wt.shape[0], :] = wt
        half_s[i * hn + wt.shape[0] : (i + 1) * hn, :] = dtw_ref[i]
        parts = [-jnp.exp(rate_ref[i]), kern_ref[i], off_ref[i : i + 1], bias_ref[i : i + 1], skip_ref[i : i + 1]]
        rest = fn - sum(v.shape[0] for v in parts)
        full_s[i * fn : (i + 1) * fn, :] = jnp.concatenate(parts + [jnp.zeros((rest, full_s.shape[1]), f32)], axis=0)
    jobs = [
        GatherBytes(here, half_s, half_ref, send, recv, 0),
        GatherBytes(here, full_s, full_ref, send, recv, GATHER_SEMS),
        Gather(here, in_ref.at[0], win_ref, send, recv, 2 * GATHER_SEMS),
        Gather(here, out_ref.at[0], wout_ref, send, recv, 3 * GATHER_SEMS),
    ]
    run_phases(jobs, [SMALL_PLAN, SMALL_PLAN, GATHER_PLAN, NEXT_PLAN])


def gather_all(xp, dtw, decay, kern, off, bias, skip, in_weight, out_weight, ident):
    layers, w, width = xp.shape
    half = (layers * (width + dtw.shape[1]), w)
    rows = decay.shape[1] + kern.shape[1] + 3
    full = (layers * (rows + -rows % 32), w)
    sems = pltpu.SemaphoreType.DMA((GATHER_SEMS * 4,))
    outs = [jax.ShapeDtypeStruct((half[0], 8 * w), bf16), jax.ShapeDtypeStruct((full[0], 8 * w), f32)]
    outs += [jax.ShapeDtypeStruct((2, 2, 4, 2) + a.shape[1:], bf16) for a in (in_weight, out_weight)]
    half, full, win, wout = pl.pallas_call(
        gather_kernel,
        out_shape=outs,
        in_specs=[INV] * 7 + [ANY] * 2,
        out_specs=[ANY] * 4,
        scratch_shapes=[pltpu.VMEM(half, bf16), pltpu.VMEM(full, f32), sems, sems],
        compiler_params=pltpu.CompilerParams(collective_id=ident, has_side_effects=True, vmem_limit_bytes=VMEM),
    )(xp, dtw, decay, kern, off, bias, skip, in_weight, out_weight)
    return half, full, win.reshape(-1, win.shape[-1]), wout.reshape(-1, wout.shape[-1])


REDUCE_SEMS = 27
FAR = (2, 1, 3, 0)


def reduce_scratch(rows, d):
    def buf(*lead, r=rows):
        return pltpu.VMEM(lead + (r, d), bf16)

    return [buf(2, 2, 4), buf(2, 2, 4), buf(4, r=rows // 2), buf(4, r=rows // 2), buf(4), buf(4), buf(3)]


class Reduce:
    def __init__(self, here, src, out, bufs, send, recv, base):
        self.here, self.src, self.out, self.send, self.recv, self.base = here, src, out, send, recv, base
        self.acc, self.rc, self.da, self.db, self.rx, self.ry, self.rz = bufs
        self.h = src.shape[4] // 2
        h = here
        self.parts = [(1 - h.y, 1 - h.x), (1 - h.y, h.x), (h.y, 1 - h.x), (h.y, h.x)]
        self.phases = (
            [self.begin, self.cross, self.pairs]
            + [functools.partial(self.side, k) for k in FAR]
            + [functools.partial(self.mine, k) for k in FAR]
            + [self.last]
        )

    def push(self, src, dst, i, device):
        return push(src, dst, self.send, self.recv, self.base + i, device)

    def own(self, part):
        y, x = self.parts[part]
        return pltpu.make_async_copy(
            self.src.at[y, x, :, self.here.c], self.acc.at[y, x], self.send.at[self.base + 23 + part]
        )

    def cores(self, part):
        y, x = self.parts[part]
        return self.push(
            self.src.at[y, x, :, 1 - self.here.c], self.rc.at[y, x], 19 + part, self.here.at(c=1 - self.here.c)
        )

    def across(self, k):
        h, z = self.here, self.here.over(k)
        block = self.acc.at[1 - h.y, 1 - h.x, z]
        return [
            self.push(block.at[pl.ds(0, self.h)], self.da.at[z], 3 + k, h.at(x=1 - h.x)),
            self.push(block.at[pl.ds(self.h, self.h)], self.db.at[z], 7 + k, h.at(y=1 - h.y)),
        ]

    def sides(self, k):
        h, z = self.here, self.here.over(k)
        return [
            self.push(self.acc.at[h.y, 1 - h.x, z], self.rx.at[z], 11 + k, h.at(x=1 - h.x)),
            self.push(self.acc.at[1 - h.y, h.x, z], self.ry.at[z], 15 + k, h.at(y=1 - h.y)),
        ]

    def line(self, k):
        h = self.here
        return self.push(self.acc.at[h.y, h.x, h.over(k)], self.rz.at[k - 1], k - 1, h.at(z=h.over(k)))

    def pair(self, part):
        y, x = self.parts[part]
        self.own(part).wait()
        self.cores(part).wait_recv()

        @pl.loop(0, 4)
        def _(z):
            self.acc[y, x, z] = self.acc[y, x, z] + self.rc[y, x, z]

    def begin(self):
        for part in range(4):
            self.cores(part).start()
            self.own(part).start()

    def cross(self):
        self.pair(0)
        for k in FAR:
            for copy in self.across(k):
                copy.start()

    def pairs(self):
        for part in (1, 2, 3):
            self.pair(part)

    def side(self, k):
        h, a, n = self.here, self.acc, self.h
        z = h.over(k)
        for copy in self.across(k):
            copy.wait_recv()
        a[1 - h.y, h.x, z, :n] = a[1 - h.y, h.x, z, :n] + self.da[z]
        a[h.y, 1 - h.x, z, n:] = a[h.y, 1 - h.x, z, n:] + self.db[z]
        for copy in self.sides(k):
            copy.start()

    def mine(self, k):
        h, a = self.here, self.acc
        z = h.over(k)
        for copy in self.sides(k):
            copy.wait_recv()
        a[h.y, h.x, z] = a[h.y, h.x, z] + self.rx[z] + self.ry[z]
        if k:
            self.line(k).start()

    def last(self):
        h = self.here
        total = self.acc[h.y, h.x, h.z].astype(f32)
        for k in (1, 3, 2):
            self.line(k).wait()
            total = total + self.rz[k - 1].astype(f32)
        self.out[...] = total
        for k in range(4):
            for copy in self.across(k) + self.sides(k):
                copy.wait_send()
            self.cores(k).wait_send()


class Reduces:
    def __init__(self, srcs, outs, scratch):
        per = len(reduce_scratch(16, 128))
        self.here = Place()
        self.jobs = [
            Reduce(self.here, src, out, scratch[per * i : per * (i + 1)], scratch[-2], scratch[-1], REDUCE_SEMS * i)
            for i, (src, out) in enumerate(zip(srcs, outs))
        ]

        self.phases = [functools.partial(self.run, i) for i in range(12)]

    def run(self, phase):
        for job in self.jobs:
            job.phases[phase]()


def reduce_parts(arrays):
    arrays = [a.reshape(2, 2, 4, 2, a.shape[0] // 32, a.shape[1]) for a in arrays]
    scratch = []
    for a in arrays:
        scratch += reduce_scratch(*a.shape[4:])
    if arrays:
        sems = pltpu.SemaphoreType.DMA((REDUCE_SEMS * len(arrays),))
        scratch += [sems, sems]
    return arrays, [jax.ShapeDtypeStruct(a.shape[4:], f32) for a in arrays], scratch


def beside(work, block, steps):
    for step in sorted(set(steps)):

        @pl.when(block == step)
        def _(step=step):
            for phase, at in enumerate(steps):
                if at == step:
                    work.phases[phase]()


SIDE_SEMS = 4


class Sides:
    def __init__(self, here, src, dst, send, recv, base):
        self.here, self.src, self.dst, self.send, self.recv, self.base = here, src, dst, send, recv, base
        self.phases = [self.begin, self.last]

    def copies(self):
        h = self.here
        dst = self.dst.at[h.y, h.x]
        to = [h.at(x=1 - h.x), h.at(y=1 - h.y), h.at(x=1 - h.x, y=1 - h.y)]
        return [push(self.src, dst, self.send, self.recv, self.base + i, p) for i, p in enumerate(to)]

    def begin(self):
        for copy in self.copies():
            copy.start()
        self.dst[self.here.y, self.here.x] = self.src[...]

    def last(self):
        for copy in self.copies():
            copy.wait()


ALL_SEMS = 6


class AllSum:
    def __init__(self, here, src, out, got, send, recv, base):
        self.here, self.src, self.out, self.got, self.send, self.recv, self.base = here, src, out, got, send, recv, base
        self.phases = [self.begin, functools.partial(self.turn, 0), functools.partial(self.turn, 1), self.along, self.last]

    def copy(self, i):
        h = self.here
        p = h.partners()[i]
        return push(self.got.at[6 + min(i, 3)], self.got.at[i], self.send, self.recv, self.base + i, p)

    def begin(self):
        self.got[6] = self.src[...]
        self.copy(0).start()

    def turn(self, i):
        self.copy(i).wait()
        self.got[7 + i] = self.got[6 + i] + self.got[i]
        self.copy(i + 1).start()

    def along(self):
        self.copy(2).wait()
        self.got[9] = self.got[8] + self.got[2]
        for i in (3, 4, 5):
            self.copy(i).start()

    def last(self):
        for i in (3, 4, 5):
            self.copy(i).wait()
        self.out[...] = self.got[9] + self.got[3] + self.got[4] + self.got[5]


def finish_kernel(cuts, small_ref, big_ref, w_ref, mixed_ref, before_ref, flow_ref, gain_ref, upper_ref,
                  flow_out, in_out, gain_out, *refs):
    outs, refs = refs[: len(cuts)], refs[len(cuts) :]
    per = len(reduce_scratch(16, 128))
    one, two, refs = refs[:per], refs[per : 2 * per], refs[2 * per :]
    w_s, gn_s, mine_s, plane_s, gains_s, got_s, send, recv, wsem = refs
    here = Place()
    greet(here.partners() + [here.at(x=1 - here.x, y=1 - here.y)])
    load = pltpu.make_async_copy(w_ref, w_s, wsem)
    load.start()
    base = 2 * REDUCE_SEMS
    small = Reduce(here, small_ref, mine_s, one, send, recv, 0)
    big = Reduce(here, big_ref, in_out, two, send, recv, REDUCE_SEMS)
    gains = AllSum(here, gains_s, gain_out, got_s, send, recv, base)
    plane = Sides(here, mine_s, plane_s, send, recv, base + ALL_SEMS)

    class Norm:
        def run(self):
            load.wait()
            depth = 512
            gn_s[...] = jnp.zeros_like(gn_s)

            @pl.loop(0, mixed_ref.shape[1] // depth)
            def _(k):
                at = pl.ds(pl.multiple_of(k * depth, depth), depth)
                gn_s[...] += dot(mixed_ref[:, at], w_s[at, :])

            gn, before, gain = gn_s[...], before_ref[...], gain_ref[...]
            inv = lax.rsqrt(jnp.mean(before * before, axis=1, keepdims=True) + norm_eps)
            scaled = before * inv
            gs = gn * gain
            flow_out[...] = flow_ref[...] + inv * (gs - scaled * jnp.mean(gs * scaled, axis=1, keepdims=True))
            gains_s[0:1, :] = jnp.sum(gn * scaled, axis=0, keepdims=True)
            gains_s[1:, :] = upper_ref[...]

        def __init__(self):
            self.phases = [self.run]

    run_phases(
        [small, big, Norm(), gains, plane],
        [SMALL_REDUCE, REDUCE_PLAN, (6,), ALL_PLAN, SIDES_PLAN],
    )
    rows, d = mine_s.shape
    layers = upper_ref.shape[0] + 1
    whole_sum = plane_s[...].reshape(4 * rows, d)
    per_layer = 4 * rows // layers
    for layer in range(layers):
        at = layer * per_layer
        for i, (cut, out) in enumerate(zip(cuts, outs)):
            v = whole_sum[at : at + cut]
            if i == 0:
                out[layer] = v.T
            elif len(out.shape) == 2:
                out[layer : layer + 1, :] = v
            else:
                out[layer] = v
            at += cut


def finish(packed, grad_in, in_full, mixed, before, flowing, gain, upper, cuts, ident):
    arrays = [a.reshape(2, 2, 4, 2, a.shape[0] // 32, a.shape[1]) for a in (packed, grad_in)]
    (rows, w), d = arrays[0].shape[4:], before.shape[1]
    layers = upper.shape[0] + 1
    outs = [jax.ShapeDtypeStruct(before.shape, f32), jax.ShapeDtypeStruct(arrays[1].shape[4:], f32),
            jax.ShapeDtypeStruct((layers, d), f32), jax.ShapeDtypeStruct((layers, w, cuts[0]), f32)]
    outs += [jax.ShapeDtypeStruct((layers, cut, w) if cut > 1 else (layers, w), f32) for cut in cuts[1:]]
    scratch = reduce_scratch(rows, w) + reduce_scratch(*arrays[1].shape[4:])
    scratch += [pltpu.VMEM(in_full.shape, bf16), pltpu.VMEM(before.shape, f32), pltpu.VMEM((rows, w), f32),
                pltpu.VMEM((2, 2, rows, w), f32), pltpu.VMEM((layers, d), f32), pltpu.VMEM((10, layers, d), f32)]
    sems = pltpu.SemaphoreType.DMA((REDUCE_SEMS * 2 + ALL_SEMS + SIDE_SEMS,))
    return pl.pallas_call(
        functools.partial(finish_kernel, cuts),
        out_shape=outs,
        in_specs=[ANY] * 3 + [INV] * 5,
        out_specs=[INV] * len(outs),
        scratch_shapes=scratch + [sems, sems, pltpu.SemaphoreType.DMA],
        compiler_params=pltpu.CompilerParams(collective_id=ident, has_side_effects=True, vmem_limit_bytes=VMEM),
    )(*arrays, in_full, mixed, before, flowing, gain, upper)


EXCHANGE_SEMS = 10


def exchange_scratch(rows, sn, c):
    h = c // 2
    sems = pltpu.SemaphoreType.DMA((EXCHANGE_SEMS,))
    return [pltpu.VMEM((sn, h), bf16)] * 4 + [
        pltpu.VMEM((rows, h), f32), pltpu.VMEM((1, rows, h), f32), pltpu.VMEM((4, sn, h), bf16),
        pltpu.VMEM((4, rows, h), f32), sems, sems,
    ]


def exchange(here, backward, rows, end_ref, sum_ref, rate_ref, out_ref, scratch):
    sent, back, got, late, gsum, msum, line, lsum, send, recv = scratch
    half = end_ref.shape[1] // 2
    mine = pl.ds(pl.multiple_of(here.c * half, half), half)
    theirs = pl.ds(pl.multiple_of((1 - here.c) * half, half), half)
    other = here.at(c=1 - here.c)
    sent[...] = end_ref[:, theirs].astype(bf16)
    msum[0] = sum_ref[:, theirs]
    one = [push(sent, got, send, recv, 0, other), push(msum.at[0], gsum, send, recv, 1, other)]
    for copy in one:
        copy.start()
    rate = rate_ref[:, mine]

    def fade(total):
        return jnp.concatenate([jnp.exp(rate * total[s : s + 1]) for s in range(rows)], axis=0)

    for copy in one:
        copy.wait()
    e_me, d_me = end_ref[:, mine], sum_ref[:, mine]
    e_it, d_it = got[...].astype(f32), gsum[...]
    first = here.c == 0
    e0, e1 = jnp.where(first, e_me, e_it), jnp.where(first, e_it, e_me)
    d0, d1 = jnp.where(first, d_me, d_it), jnp.where(first, d_it, d_me)
    chip = e0 + fade(d0) * e1 if backward else fade(d1) * e0 + e1
    line[3] = chip.astype(bf16)
    lsum[3] = d0 + d1
    two = []
    for k in (1, 2, 3):
        two.append(push(line.at[3], line.at[k - 1], send, recv, 2 + 2 * k, here.at(z=here.over(k))))
        two.append(push(lsum.at[3], lsum.at[k - 1], send, recv, 3 + 2 * k, here.at(z=here.over(k))))
    for copy in two:
        copy.start()
    for copy in two:
        copy.wait()
    state = jnp.zeros_like(chip)
    for k in (1, 2, 3) if backward else (3, 2, 1):
        at = lax.rem(here.z + 4 - k, 4)
        e, d = line[k - 1].astype(f32), lsum[k - 1]
        use = at > here.z if backward else at < here.z
        state = jnp.where(use, fade(d) * state + e, state)
    if backward:
        s1, s0 = state, e1 + fade(d1) * state
    else:
        s0, s1 = state, fade(d0) * state + e0
    out_ref[:, mine] = jnp.where(first, s0, s1)
    back[...] = jnp.where(first, s1, s0).astype(bf16)
    three = push(back, late, send, recv, 2, other)
    three.start()
    three.wait()
    out_ref[:, theirs] = late[...].astype(f32)


def carried_in(ends, sums, rate, axis, backward):
    n = lax.axis_size(axis)
    rows = sums.shape[0]
    ns = rate.shape[0]

    def fade(total):
        return jnp.exp(total[:, None, :] * rate[None])

    def moved(v, shift):
        if backward:
            pairs = [(i, i - shift) for i in range(shift, n)]
        else:
            pairs = [(i, i + shift) for i in range(n - shift)]
        return lax.ppermute(v, axis, pairs)

    def shifted(e, s, shift):
        return moved(e.astype(bf16), shift).astype(f32), moved(s, shift)

    ends = ends.reshape(rows, ns, -1)
    ends, sums = shifted(ends, sums, 1)
    shift = 1
    while shift < n - 1:
        e, s = shifted(ends, sums, shift)
        ends = fade(sums) * e + ends
        sums = sums + s
        shift *= 2
    return ends.reshape(rows * ns, -1)


def body(
    tokens, boundaries, norm_gain, in_weight, out_weight, conv_weight, conv_bias, xproj_weight,
    dtproj_weight, dt_bias, decay_log, skip_gain, cotangent,
):
    rows, length, d = tokens.shape
    layers = norm_gain.shape[0]
    both = ("rows", "bytes")
    n = rows * length
    place = lax.axis_index("bytes") * length + jnp.arange(length, dtype=jnp.int32)
    reached = boundaries[:, None, :] <= place[None, :, None]
    starts = jnp.max(jnp.where(reached, boundaries[:, None, :], 0), axis=2)
    renewed = jnp.any(boundaries[:, None, :] == place[None, :, None], axis=2)
    kill = jnp.broadcast_to(jnp.where(renewed, KILL, 0.0).reshape(n, 1), (n, 128)).astype(f32)
    taps = conv_weight.shape[1]
    masks = jnp.stack(
        [
            jnp.broadcast_to((place[None, :] - lag >= starts).astype(f32).reshape(n, 1), (n, 128))
            for lag in range(1, taps)
        ]
    )
    fast = (lax.axis_size("rows"), lax.axis_size("bytes")) == (4, 8)
    if fast:
        half, full, first_in, first_out = gather_all(
            xproj_weight, dtproj_weight, decay_log, conv_weight, conv_bias, dt_bias, skip_gain, in_weight, out_weight, 1
        )
    else:
        half = jnp.concatenate([xproj_weight.transpose(0, 2, 1), dtproj_weight], axis=1)
        full = jnp.concatenate(
            [-jnp.exp(decay_log), conv_weight, conv_bias[:, None], dt_bias[:, None], skip_gain[:, None]], axis=1
        )
        half = lax.all_gather(half, "bytes", axis=2, tiled=True)
        full = lax.all_gather(full, "bytes", axis=2, tiled=True)
    ns = decay_log.shape[1]
    rank = dtproj_weight.shape[1]
    width = xproj_weight.shape[2]
    channels = full.shape[-1]
    mixer = Mixer(layers, rows, length, channels, ns, rank, taps)
    params = []
    for i in range(0 if fast else layers):
        rest = full[i, ns + taps :]
        params.append(
            dict(
                xproj=half[i, :width], dtproj=half[i, width:], conv_w=full[i, ns : ns + taps], conv_b=rest[:1],
                dt_b=rest[1:2], skip=rest[2:3], rate=full[i, :ns],
            )
        )
    if fast:
        in_fulls, out_fulls = {0: first_in}, {0: first_out}
    else:
        in_fulls = {i: lax.all_gather(in_weight[i], both, axis=0, tiled=True) for i in range(layers)}
        out_fulls = {i: lax.all_gather(out_weight[i], both, axis=0, tiled=True) for i in range(layers)}
    size = lax.axis_size("bytes")
    ahead = [(i, i + 1) for i in range(size - 1)]
    behind = [(i + 1, i) for i in range(size - 1)]
    current = tokens.astype(f32).reshape(n, d)
    saved = []
    for i in range(layers):
        p = None if fast else params[i]
        if fast:
            (normed, x, z, halo, act, rank_t, bb, cc, delta, total, y, gated, keep), whole_w = mixer.forward(
                i, current, norm_gain[i][None], in_fulls[i], half, full, masks, kill,
                ([(out_weight, i)] if i else []) + [(in_weight, j) for j in range(i + 1, min(i + 2, layers))], 2 + i,
            )
            m = dict(rank_t=rank_t, bb=bb, cc=cc)
            if i:
                out_fulls[i] = whole_w[0]
            if i + 1 < layers:
                in_fulls[i + 1] = whole_w[-1]
        else:
            normed = (
                current * lax.rsqrt(jnp.mean(current * current, axis=-1, keepdims=True) + norm_eps) * norm_gain[i]
            ).astype(bf16)
            projected = dot_nt(normed, in_fulls[i])
            tail = projected.reshape(rows, length, -1)[:, length - 8 :, :channels].astype(bf16)
            halo = lax.ppermute(tail, "bytes", ahead).reshape(8 * rows, channels)
            act, m = mixer.conv(projected, halo, p, masks)
            delta, end, total = mixer.ends(act, m, p, kill)
            start = carried_in(end, total, p["rate"], "bytes", False)
            y, gated, keep = mixer.scan(act, delta, projected, m, p, kill, start)
            x = z = projected
        saved.append((current, normed, x, z, halo, act, m, delta, total, y, gated, keep))
        current = current + dot(gated, out_fulls[i])
    flowing = cotangent.astype(f32).reshape(n, d)
    big, small, gains = [], [], []
    waiting, ready = [], []
    for i in reversed(range(layers)):
        p = None if fast else params[i]
        in_full, out_full = in_fulls[i], out_fulls[i]
        before, normed, x, z, halo, act, m, delta, total, y, gated, keep = saved[i]
        down = flowing.astype(bf16)
        grad_out = lax.dot_general(gated, down, (((0,), (0,)), ((), ())), preferred_element_type=f32).astype(bf16)
        gg = dot_nt(down, out_full)
        if fast:
            waiting.append(grad_out)
            (mixed, pieces), done = mixer.backward(
                i, gg, x, z, halo, y, act, delta, total, m, half, full, masks, kill, keep, waiting, 10 + i
            )
            ready += done
        else:
            gy, gz, gend = mixer.back_ends(gg, z, y, delta, m, p, kill)
            gstart = carried_in(gend, total, p["rate"], "bytes", True)
            gact, gproj, gproj_t, gdtw, gbias, grate, gskip = mixer.back(act, delta, gy, m, p, kill, keep, gstart)
            gx, edge, gxp, gkern, goff = mixer.conv_back(x, halo, p, masks, act, gact, gproj, gproj_t)
            late = lax.ppermute(edge.astype(bf16), "bytes", behind).astype(f32).reshape(rows, 8, channels)
            gx = (
                (gx.reshape(rows, length, channels) + jnp.pad(late, ((0, 0), (length - 8, 0), (0, 0))))
                .reshape(n, channels)
                .astype(bf16)
            )
            mixed = jnp.concatenate([gx, gz], axis=1)
            pieces = jnp.concatenate([gxp, gdtw, grate, gkern, goff, gbias, gskip], axis=0)
        grad_in = lax.dot_general(mixed, normed, (((0,), (0,)), ((), ())), preferred_element_type=f32).astype(bf16)
        small.append(pieces)
        waiting = [grad_in]
        if fast and i == 0:
            break
        gn = dot(mixed, in_full)
        inv = lax.rsqrt(jnp.mean(before * before, axis=-1, keepdims=True) + norm_eps)
        scaled = before * inv
        gains.append(jnp.sum(gn * scaled, axis=0))
        gs = gn * norm_gain[i]
        flowing = flowing + inv * (gs - scaled * jnp.mean(gs * scaled, axis=-1, keepdims=True))
        if not fast:
            big.append([lax.psum_scatter(g, both, scatter_dimension=0, tiled=True).astype(f32) for g in (grad_in, grad_out)])
    cuts = [width, rank, ns, taps, 1, 1, 1]
    if fast:
        packed = jnp.stack(small[::-1])
        packed = packed.reshape(4, layers * packed.shape[1] // 4, size, channels // size).transpose(0, 2, 1, 3)
        flowing, last_in, gain_total, *parts = finish(
            packed.reshape(-1, channels // size), grad_in, in_full, mixed, before, flowing, norm_gain[0][None],
            jnp.stack(gains[::-1]), cuts, 9,
        )
        ready.append(last_in)
        big = [(ready[2 * i + 1], ready[2 * i]) for i in range(layers)]
    else:
        packed = jnp.stack(small[::-1]).astype(bf16)
        packed = lax.psum_scatter(packed, "bytes", scatter_dimension=2, tiled=True)
        packed = lax.psum(packed, "rows").astype(f32)
        gain_total = lax.psum(jnp.stack(gains[::-1]), both)
        parts, at = [], 0
        for cut in cuts:
            parts.append(packed[:, at] if cut == 1 else packed[:, at : at + cut])
            at += cut
        parts[0] = parts[0].transpose(0, 2, 1)
    big = big[::-1]
    return (
        current.reshape(rows, length, d),
        flowing.reshape(rows, length, d),
        gain_total,
        jnp.stack([b[0] for b in big]),
        jnp.stack([b[1] for b in big]),
        parts[3],
        parts[4],
        parts[0],
        parts[1],
        parts[5],
        parts[2],
        parts[6],
    )


def solution(mesh):
    split = P("rows", "bytes", None)
    shared = P(None, ("rows", "bytes"), None)
    in_specs = (
        split, P("rows", None), P(), shared, shared, P(None, None, "bytes"), P(None, "bytes"),
        P(None, "bytes", None), P(None, None, "bytes"), P(None, "bytes"), P(None, None, "bytes"),
        P(None, "bytes"), split,
    )
    out_specs = (
        split, split, P(), shared, shared, P(None, None, "bytes"), P(None, "bytes"), P(None, "bytes", None),
        P(None, None, "bytes"), P(None, "bytes"), P(None, None, "bytes"), P(None, "bytes"),
    )
    return jax.shard_map(body, mesh=mesh, in_specs=in_specs, out_specs=out_specs, check_vma=False)
```

time: 1430 us -> 486 us (0.34)
  waiting for transfers between devices: 704 us -> 0 us
  local copies, waits for them, and re-layouts: 110 us -> 14.5 us
  starting transfers between devices: 87.4 us -> 0 us
  Pallas kernels: 333 us -> 419 us
  blocking collectives: 56.2 us -> 0 us
  other arithmetic: 39.8 us -> 9.06 us
  matrix products: 66.3 us -> 38.6 us
  between operations: 16 us -> 1.24 us
    reduce_scatter x5 -> x0, waiting for transfers between devices: 577 us -> none  [the longest x2 301 us: body(): lax.psum_scatter(grad_in, both, scatter_dimension=0, tiled=True).astype(f32)]
    pallas_call x0 -> x2, Pallas kernels: none -> 135 us  [the longest x1 73.1 us: gather_all(): pl.pallas_call(gather_kernel, out_shape=outs, in_specs=[INV] * 7 + [ANY]...]
    ppermute x32 -> x0, starting transfers between devices: 86.7 us -> none  [the longest x28 79.6 us: moved(): return lax.ppermute(v, axis, pairs)]
    all_gather x5 -> x0, waiting for transfers between devices: 78 us -> none  [the longest x2 78 us: body(): lax.all_gather(in_weight[i], both, axis=0, tiled=True)]
    pallas_call x12 -> x4, Pallas kernels: 333 us -> 284 us  [call(): pl.pallas_call(body, grid=(blocks,), in_specs=ins, out_specs=[spec for sp...]
    ppermute x32 -> x0, waiting for transfers between devices: 48.2 us -> none  [the longest x28 45.6 us: moved(): return lax.ppermute(v, axis, pairs)]
    unnamed x295 -> x59, local copies, waits for them, and re-layouts: 51.7 us -> 10.6 us
    psum x1 -> x0, blocking collectives: 38.8 us -> none  [body(): gain_total = lax.psum(jnp.stack(gains), both)]
  transfers between devices with their start and end apart: 43 -> 0, of which waited for: 24 -> 0; matrix products, arithmetic and copies ran while one was open for 9% -> 0% of each run, Pallas kernels for 7% -> 0%
where the time goes in v1:
time: 486 us; the launch traced here: 482 us
  Pallas kernels  419 us (86%)
  matrix products  38.6 us (8%)
  local copies, waits for them, and re-layouts  14.5 us (3%)
  other arithmetic  9.06 us (2%)
    pallas_call x4, Pallas kernels, call(): pl.pallas_call(body, grid=(blocks,), in_specs=ins, out_specs=[spec for sp...  284 us
    pallas_call x1, Pallas kernels, gather_all(): pl.pallas_call(gather_kernel, out_shape=outs, in_specs=[INV] * 7 + [ANY]...  73.1 us
    pallas_call x1, Pallas kernels, finish(): pl.pallas_call(functools.partial(finish_kernel, cuts), out_shape=outs, in...  61.6 us
    dot_general x3, matrix products, dot(): return jnp.dot(a, b, preferred_element_type=f32)  15.4 us
    dot_general x2, matrix products, body(): lax.dot_general(mixed, normed, (((0,), (0,)), ((), ())), preferred_elemen...  11.2 us
    unnamed x59, local copies, waits for them, and re-layouts  10.6 us

profile of v1, /device:TPU:0, one launch (start us, length us, event | category | flops | bytes accessed | tf_op | source)
XLA Modules:
  0.0 482.5 jit_solution(13299522096849472749)
XLA Ops:
  0.7 0.8 compare_reduce_fusion
  1.4 0.8 select_reduce_fusion
  2.2 1.4 fusion.6
  3.6 0.8 broadcast_in_dim.23.refs_8_.refs_5_
  4.7 0.8 pad_maximum_fusion.3.refs_6_.refs_18_
  5.4 1.7 copy.29.xp_ref
  7.1 2.1 bitcast_convert_fusion.refs_0_.before_ref
  9.2 73.1 %shard_map.220 = (bf16[320,2048]{1,0:T(8,128)(2,1)}, f32[64,2048]{1,0:T(8,128)}, bf16[2,2,4,2,128,1024]{5,4,3,2,1,0:T(8,128)(2,1)}, bf16[2,2,4,2,64,1024]{5,4,3,2,1,0:T(8,128)(2,1)}) custom-call(bf16[2,256,96]{2,1,0:T(8,128)(2,1)} %copy.29.xp_ref, bf16[2,64,256]{2,1,0:T(8,128)(2,1)} %dtw_ref.1, f32[2,16,256]{2,1,0:T(8,128)} %rate_ref.1, ...), custom_call_target="tpu_custom_call" | custom-call | tf_op jit(solution)/shard_map/pallas_call | solution.py:1130
  82.3 72.3 %shard_map.221 = (bf16[256,1024]{1,0:T(8,128)(2,1)}, bf16[256,2048]{1,0:T(8,128)(2,1)}, f32[256,2048]{1,0:T(8,128)}, bf16[16,2048]{1,0:T(8,128)(2,1)}, f32[256,2...) custom-call(f32[256,1024]{1,0:T(8,128)} %bitcast_convert_fusion.refs, ...), custom_call_target="tpu_custom_call" | custom-call | tf_op jit(solution)/shard_map/pallas_call | solution.py:666
  154.7 3.5 multiply_reduce_fusion.2
  158.1 62.7 %shard_map.222 = (bf16[256,1024]{1,0:T(8,128)(2,1)}, bf16[256,2048]{1,0:T(8,128)(2,1)}, f32[256,2048]{1,0:T(8,128)}, bf16[16,2048]{1,0:T(8,128)(2,1)}, f32[256,2...) custom-call(f32[256,1024]{1,0:T(8,128)} %get-tuple-element.142.refs_, ...), custom_call_target="tpu_custom_call" | custom-call | tf_op jit(solution)/shard_map/pallas_call | solution.py:666
  220.9 4.9 %convolution_add_fusion = f32[256,1024]{1,0:T(8,128)} fusion(f32[256,1024]{1,0:T(8,128)S(1)} %copy-done.4, bf16[256,2048]{1,0:T(8,128)(2,1)} %get-tuple-element.67, bf16[2048,1024]{1,0:T(8,128)(2,1)} %bitcast.83), kind=kOutput, calls=%fused_computation.6 | convolution fusion | flops 1074003968 | bytes 7340032 | tf_op jit(solution)/shard_map/dot_general | solution.py:29
  225.8 2.7 convolution_bitcast_fusion.refs_0_
  228.5 3.3 convolution_convert_fusion.3
  231.8 70.3 %shard_map.223 = (bf16[256,4096]{1,0:T(8,128)(2,1)}, bf16[192,2048]{1,0:T(8,128)(2,1)}, f32[64,1024]{1,0:T(8,128)}) custom-call(f32[256,2048]{1,0:T(8,128)} %convolution_bitcast_fusion.refs_0_, f32[256,2048]{1,0:T(8,128)} %get-tuple-element.69.refs_1_, bf16[256,2048]{1,0:T(8,128)(2,1)} %get-tuple-element.70.refs_2_, ...), custom_call_target="tpu_custom_call" | custom-call | tf_op jit(solution)/shard_map/pallas_call | solution.py:666
  302.1 7.1 %multiply_reduce_fusion = (f32[1024]{0:T(1024)}, f32[256]{0:T(256)S(1)}, f32[256,1024]{1,0:T(8,128)S(1)}) fusion(f32[256,1024]{1,0:T(8,128)S(1)} %copy-done.4, f32[256]{0:T(256)S(1)} %add_rsqrt_fusion, f32[1024]{0:T(1024)S(1)} %bitcast.80, bf16[256,4096]{1,0:T(8,128)(2,1)} %get-tuple-element.80, bf16[4096,1024]{1,0:T(8,128)(2,1)} %bitcast.63), kind=kOutput, calls=%fused_computation.9 | convolution fusion | flops 2149055232 | bytes 12593152 | tf_op jit(solution)/shard_map/dot_general | solution.py:29
  309.5 2.6 fusion.1.refs_0_
  312.2 3.3 convolution_convert_fusion.2
  315.5 5.6 %convolution_convert_fusion.1 = bf16[4096,1024]{1,0:T(8,128)(2,1)} fusion(bf16[256,4096]{1,0:T(8,128)(2,1)S(1)} %copy-done.5, bf16[256,1024]{1,0:T(8,128)(2,1)S(1)} %copy-done.11), kind=kOutput, calls=%fused_computation.1 | convolution fusion | flops 2151677952 | bytes 11010048 | tf_op jit(solution)/shard_map/dot_general | solution.py:1635
  321.1 79.1 %shard_map.224 = (bf16[256,4096]{1,0:T(8,128)(2,1)}, bf16[192,2048]{1,0:T(8,128)(2,1)}, f32[128,1024]{1,0:T(8,128)}, f32[64,1024]{1,0:T(8,128)}) custom-call(f32[256,2048]{1,0:T(8,128)} %fusion.1.refs_0_, f32[256,2048]{1,0:T(8,128)} %get-tuple-element.81.refs_1_, bf16[256,2048]{1,0:T(8,128)(2,1)} %get-tuple-element.82.refs_2_, ...), custom_call_target="tpu_custom_call" | custom-call | tf_op jit(solution)/shard_map/pallas_call | solution.py:666
  400.2 1.3 pad_maximum_fusion
  402.1 1.5 copy.31
  403.6 0.8 pad_maximum_fusion.2
  404.4 5.6 %convolution_convert_fusion = bf16[4096,1024]{1,0:T(8,128)(2,1)} fusion(bf16[256,4096]{1,0:T(8,128)(2,1)S(1)} %copy-done.1, bf16[256,1024]{1,0:T(8,128)(2,1)S(1)} %copy-done.10), kind=kOutput, calls=%fused_computation | convolution fusion | flops 2151677952 | bytes 11010048 | tf_op jit(solution)/shard_map/dot_general | solution.py:1635
  410.1 61.6 %shard_map.225 = (f32[256,1024]{1,0:T(8,128)}, f32[128,1024]{1,0:T(8,128)}, f32[2,1024]{1,0:T(2,128)}, f32[2,256,96]{2,1,0:T(8,128)}, f32[2,64,256]{2,1,0:T(8,12...) custom-call(bf16[2,2,4,2,96,256]{5,4,3,2,1,0:T(8,128)(2,1)} %bitcast, ...), custom_call_target="tpu_custom_call" | custom-call | tf_op jit(solution)/shard_map/pallas_call | solution.py:1421
  471.8 1.8 copy.32
  473.6 2.1 pad_maximum_fusion.1
  475.7 2.3 copy.43
  478.0 0.6 copy.44
  478.6 0.6 copy.45
  479.8 0.7 copy.47
  481.0 0.6 copy.49
  (62 shorter events, 3.0 us)
Async XLA Ops:
  82.3 72.3 %copy-start.2 = (f32[256,1024]{1,0:T(8,128)S(1)}, f32[256,1024]{1,0:T(8,128)}, u32[]{:S(2)}) copy-start(f32[256,1024]{1,0:T(8,128)} %bitcast_convert_fusion.refs_0_.before_ref) | copy-start | bytes 3145732
  82.3 72.3 %copy-start.3 = (bf16[2,2,4,2,64,1024]{5,4,3,2,1,0:T(8,128)(2,1)S(1)}, bf16[2,2,4,2,64,1024]{5,4,3,2,1,0:T(8,128)(2,1)}, u32[]{:S(2)}) copy-start(bf16[2,2,4,2,64,1024]{5,4,3,2,1,0:T(8,128)(2,1)} %get-tuple-element.65) | copy-start | bytes 12582916
  158.1 62.7 %copy-start.4 = (f32[256,1024]{1,0:T(8,128)S(1)}, f32[256,1024]{1,0:T(8,128)}, u32[]{:S(2)}) copy-start(f32[256,1024]{1,0:T(8,128)} %get-tuple-element.142.refs_0_) | copy-start | bytes 3145732
  220.9 4.9 %copy-start.8 = (bf16[2,128,1024]{2,1,0:T(8,128)(2,1)S(1)}, bf16[2,128,1024]{2,1,0:T(8,128)(2,1)}, u32[]{:S(2)}) copy-start(bf16[2,128,1024]{2,1,0:T(8,128)(2,1)} %param.25) | copy-start | bytes 1572868
  220.9 4.9 %copy-start.23 = (bf16[2,2,4,2,64,1024]{5,4,3,2,1,0:T(8,128)(2,1)S(1)}, bf16[2,2,4,2,64,1024]{5,4,3,2,1,0:T(8,128)(2,1)}, u32[]{:S(2)}) copy-start(bf16[2,2,4,2,64,1024]{5,4,3,2,1,0:T(8,128)(2,1)} %get-tuple-element.68) | copy-start | bytes 12582916
  225.8 2.7 copy-start.7
  231.8 70.3 %copy-start.16 = (f32[1,1024]{1,0:T(1,128)S(1)}, f32[1,1024]{1,0:T(1,128)}, u32[]{:S(2)}) copy-start(f32[1,1024]{1,0:T(1,128)} %get-tuple-element.136.refs_1_) | copy-start | bytes 12292
  309.5 5.9 %copy-start = (f32[256,1024]{1,0:T(8,128)}, f32[256,1024]{1,0:T(8,128)S(1)}, u32[]{:S(2)}) copy-start(f32[256,1024]{1,0:T(8,128)S(1)} %multiply_add_fusion.flow_ref) | copy-start | bytes 3145732
  309.5 2.6 copy-start.6
  312.2 3.3 copy-start.5
  312.2 3.3 copy-start.11
  321.1 79.1 %copy-start.9 = (bf16[192,2048]{1,0:T(8,128)(2,1)S(1)}, bf16[192,2048]{1,0:T(8,128)(2,1)}, u32[]{:S(2)}) copy-start(bf16[192,2048]{1,0:T(8,128)(2,1)} %get-tuple-element.94) | copy-start | bytes 2359300
  400.2 3.4 copy-start.13
  400.2 3.4 copy-start.14
  401.5 2.9 copy-start.1
  401.6 2.9 copy-start.10
  410.1 63.5 %copy-start.12 = (f32[128,1024]{1,0:T(8,128)S(1)}, f32[128,1024]{1,0:T(8,128)}, u32[]{:S(2)}) copy-start(f32[128,1024]{1,0:T(8,128)} %get-tuple-element.100) | copy-start | bytes 1572868
  471.7 6.3 %copy-start.19 = (f32[2,1024]{1,0:T(2,128)S(1)}, f32[2,1024]{1,0:T(2,128)}, u32[]{:S(2)}) copy-start(f32[2,1024]{1,0:T(2,128)} %get-tuple-element.162) | copy-start | bytes 24580
  471.7 6.9 %copy-start.18 = (f32[2,4,256]{2,1,0:T(4,128)S(1)}, f32[2,4,256]{2,1,0:T(4,128)}, u32[]{:S(2)}) copy-start(f32[2,4,256]{2,1,0:T(4,128)} %get-tuple-element.165) | copy-start | bytes 24580
  471.7 7.5 %copy-start.22 = (f32[2,256]{1,0:T(2,128)S(1)}, f32[2,256]{1,0:T(2,128)}, u32[]{:S(2)}) copy-start(f32[2,256]{1,0:T(2,128)} %get-tuple-element.166) | copy-start | bytes 6148
  471.7 8.0 %copy-start.15 = (f32[2,64,256]{2,1,0:T(8,128)S(1)}, f32[2,64,256]{2,1,0:T(8,128)}, u32[]{:S(2)}) copy-start(f32[2,64,256]{2,1,0:T(8,128)} %get-tuple-element.168) | copy-start | bytes 393220
  471.8 8.7 %copy-start.21 = (f32[2,256]{1,0:T(2,128)S(1)}, f32[2,256]{1,0:T(2,128)}, u32[]{:S(2)}) copy-start(f32[2,256]{1,0:T(2,128)} %get-tuple-element.169) | copy-start | bytes 6148
  471.8 9.3 %copy-start.17 = (f32[2,16,256]{2,1,0:T(8,128)S(1)}, f32[2,16,256]{2,1,0:T(8,128)}, u32[]{:S(2)}) copy-start(f32[2,16,256]{2,1,0:T(8,128)} %get-tuple-element.170) | copy-start | bytes 98308
  471.8 9.9 %copy-start.20 = (f32[2,256]{1,0:T(2,128)S(1)}, f32[2,256]{1,0:T(2,128)}, u32[]{:S(2)}) copy-start(f32[2,256]{1,0:T(2,128)} %get-tuple-element.171) | copy-start | bytes 6148

commit v2 on v1

--- a/solution.py
+++ b/solution.py
@@ -269,7 +269,7 @@
     def _():
         greet(here.partners() + [here.ring(1), here.ring(-1)])
         proj_s[...] = jnp.zeros_like(proj_s)
-        h = h_ref[...]
+        h = h_ref[...].astype(f32)
         normed_ref[...] = (
             h * lax.rsqrt(jnp.mean(h * h, axis=1, keepdims=True) + norm_eps) * gain_ref[...]
         ).astype(bf16)
@@ -1104,9 +1104,9 @@
     layers = xp_ref.shape[0]
     hn, fn = half_s.shape[0] // layers, full_s.shape[0] // layers
     for i in range(layers):
-        wt = xp_ref[i].astype(f32).T.astype(bf16)
-        half_s[i * hn : i * hn + wt.shape[0], :] = wt
-        half_s[i * hn + wt.shape[0] : (i + 1) * hn, :] = dtw_ref[i]
+        width = xp_ref.shape[1]
+        half_s[i * hn : i * hn + width, :] = xp_ref[i]
+        half_s[i * hn + width : (i + 1) * hn, :] = dtw_ref[i]
         parts = [-jnp.exp(rate_ref[i]), kern_ref[i], off_ref[i : i + 1], bias_ref[i : i + 1], skip_ref[i : i + 1]]
         rest = fn - sum(v.shape[0] for v in parts)
         full_s[i * fn : (i + 1) * fn, :] = jnp.concatenate(parts + [jnp.zeros((rest, full_s.shape[1]), f32)], axis=0)
@@ -1120,7 +1120,7 @@
 
 
 def gather_all(xp, dtw, decay, kern, off, bias, skip, in_weight, out_weight, ident):
-    layers, w, width = xp.shape
+    layers, width, w = xp.shape
     half = (layers * (width + dtw.shape[1]), w)
     rows = decay.shape[1] + kern.shape[1] + 3
     full = (layers * (rows + -rows % 32), w)
@@ -1375,7 +1375,7 @@
                 at = pl.ds(pl.multiple_of(k * depth, depth), depth)
                 gn_s[...] += dot(mixed_ref[:, at], w_s[at, :])
 
-            gn, before, gain = gn_s[...], before_ref[...], gain_ref[...]
+            gn, before, gain = gn_s[...], before_ref[...].astype(f32), gain_ref[...]
             inv = lax.rsqrt(jnp.mean(before * before, axis=1, keepdims=True) + norm_eps)
             scaled = before * inv
             gs = gn * gain
@@ -1396,11 +1396,9 @@
     per_layer = 4 * rows // layers
     for layer in range(layers):
         at = layer * per_layer
-        for i, (cut, out) in enumerate(zip(cuts, outs)):
+        for cut, out in zip(cuts, outs):
             v = whole_sum[at : at + cut]
-            if i == 0:
-                out[layer] = v.T
-            elif len(out.shape) == 2:
+            if len(out.shape) == 2:
                 out[layer : layer + 1, :] = v
             else:
                 out[layer] = v
@@ -1412,8 +1410,8 @@
     (rows, w), d = arrays[0].shape[4:], before.shape[1]
     layers = upper.shape[0] + 1
     outs = [jax.ShapeDtypeStruct(before.shape, f32), jax.ShapeDtypeStruct(arrays[1].shape[4:], f32),
-            jax.ShapeDtypeStruct((layers, d), f32), jax.ShapeDtypeStruct((layers, w, cuts[0]), f32)]
-    outs += [jax.ShapeDtypeStruct((layers, cut, w) if cut > 1 else (layers, w), f32) for cut in cuts[1:]]
+            jax.ShapeDtypeStruct((layers, d), f32)]
+    outs += [jax.ShapeDtypeStruct((layers, cut, w) if cut > 1 else (layers, w), f32) for cut in cuts]
     scratch = reduce_scratch(rows, w) + reduce_scratch(*arrays[1].shape[4:])
     scratch += [pltpu.VMEM(in_full.shape, bf16), pltpu.VMEM(before.shape, f32), pltpu.VMEM((rows, w), f32),
                 pltpu.VMEM((2, 2, rows, w), f32), pltpu.VMEM((layers, d), f32), pltpu.VMEM((10, layers, d), f32)]
@@ -1544,7 +1542,7 @@
     fast = (lax.axis_size("rows"), lax.axis_size("bytes")) == (4, 8)
     if fast:
         half, full, first_in, first_out = gather_all(
-            xproj_weight, dtproj_weight, decay_log, conv_weight, conv_bias, dt_bias, skip_gain, in_weight, out_weight, 1
+            xproj_weight.transpose(0, 2, 1), dtproj_weight, decay_log, conv_weight, conv_bias, dt_bias, skip_gain, in_weight, out_weight, 1
         )
     else:
         half = jnp.concatenate([xproj_weight.transpose(0, 2, 1), dtproj_weight], axis=1)
@@ -1581,7 +1579,7 @@
         p = None if fast else params[i]
         if fast:
             (normed, x, z, halo, act, rank_t, bb, cc, delta, total, y, gated, keep), whole_w = mixer.forward(
-                i, current, norm_gain[i][None], in_fulls[i], half, full, masks, kill,
+                i, current if i else tokens.reshape(n, d), norm_gain[i][None], in_fulls[i], half, full, masks, kill,
                 ([(out_weight, i)] if i else []) + [(in_weight, j) for j in range(i + 1, min(i + 2, layers))], 2 + i,
             )
             m = dict(rank_t=rank_t, bb=bb, cc=cc)
@@ -1650,7 +1648,7 @@
         packed = jnp.stack(small[::-1])
         packed = packed.reshape(4, layers * packed.shape[1] // 4, size, channels // size).transpose(0, 2, 1, 3)
         flowing, last_in, gain_total, *parts = finish(
-            packed.reshape(-1, channels // size), grad_in, in_full, mixed, before, flowing, norm_gain[0][None],
+            packed.reshape(-1, channels // size), grad_in, in_full, mixed, tokens.reshape(n, d), flowing, norm_gain[0][None],
             jnp.stack(gains[::-1]), cuts, 9,
         )
         ready.append(last_in)
@@ -1664,7 +1662,6 @@
         for cut in cuts:
             parts.append(packed[:, at] if cut == 1 else packed[:, at : at + cut])
             at += cut
-        parts[0] = parts[0].transpose(0, 2, 1)
     big = big[::-1]
     return (
         current.reshape(rows, length, d),
@@ -1674,7 +1671,7 @@
         jnp.stack([b[1] for b in big]),
         parts[3],
         parts[4],
-        parts[0],
+        parts[0].transpose(0, 2, 1),
         parts[1],
         parts[5],
         parts[2],

time: 486 us -> 486 us (level); the launches traced: 482 us -> 477 us
    unnamed x59 -> x62, local copies, waits for them, and re-layouts: 10.6 us -> 7.79 us
where the time goes in v2:
time: 486 us; the launch traced here: 477 us
  Pallas kernels  418 us (86%)
  matrix products  38.7 us (8%)
  local copies, waits for them, and re-layouts  11.7 us (2%)
  other arithmetic  7.05 us (1%)
    pallas_call x4, Pallas kernels, call(): pl.pallas_call(body, grid=(blocks,), in_specs=ins, out_specs=[spec for sp...  283 us
    pallas_call x1, Pallas kernels, gather_all(): pl.pallas_call(gather_kernel, out_shape=outs, in_specs=[INV] * 7 + [ANY]...  73 us
    pallas_call x1, Pallas kernels, finish(): pl.pallas_call(functools.partial(finish_kernel, cuts), out_shape=outs, in...  61.4 us
    dot_general x3, matrix products, dot(): return jnp.dot(a, b, preferred_element_type=f32)  15.6 us
    dot_general x2, matrix products, body(): lax.dot_general(mixed, normed, (((0,), (0,)), ((), ())), preferred_elemen...  11.2 us

profile of v2, /device:TPU:0, one launch (start us, length us, event | category | flops | bytes accessed | tf_op | source)
XLA Modules:
  0.0 476.8 jit_solution(3244458755243071802)
XLA Ops:
  0.7 0.8 compare_reduce_fusion
  1.4 0.8 select_reduce_fusion
  2.2 1.4 fusion.6
  3.6 0.8 broadcast_in_dim.23.refs_8_.refs_5_
  4.7 0.8 pad_maximum_fusion.3.refs_6_.refs_18_
  5.4 73.0 %shard_map.220 = (bf16[320,2048]{1,0:T(8,128)(2,1)}, f32[64,2048]{1,0:T(8,128)}, bf16[2,2,4,2,128,1024]{5,4,3,2,1,0:T(8,128)(2,1)}, bf16[2,2,4,2,64,1024]{5,4,3,2,1,0:T(8,128)(2,1)}) custom-call(bf16[2,96,256]{2,1,0:T(8,128)(2,1)} %bitcast.84, bf16[2,64,256]{2,1,0:T(8,128)(2,1)} %dtw_ref.1, f32[2,16,256]{2,1,0:T(8,128)} %rate_ref.1, f32[2,4,256]{2,1,0:T(4,128)} %kern_ref.1, ...), custom_call_target="tpu_custom_call" | custom-call | tf_op jit(solution)/shard_map/pallas_call | solution.py:1130
  78.5 71.4 %shard_map.221 = (bf16[256,1024]{1,0:T(8,128)(2,1)}, bf16[256,2048]{1,0:T(8,128)(2,1)}, f32[256,2048]{1,0:T(8,128)}, bf16[16,2048]{1,0:T(8,128)(2,1)}, f32[256,2...) custom-call(bf16[256,1024]{1,0:T(8,128)(2,1)} %bitcast.71, ...), custom_call_target="tpu_custom_call" | custom-call | tf_op jit(solution)/shard_map/pallas_call | solution.py:666
  149.9 3.5 multiply_reduce_fusion.2
  153.4 62.7 %shard_map.222 = (bf16[256,1024]{1,0:T(8,128)(2,1)}, bf16[256,2048]{1,0:T(8,128)(2,1)}, f32[256,2048]{1,0:T(8,128)}, bf16[16,2048]{1,0:T(8,128)(2,1)}, f32[256,2...) custom-call(f32[256,1024]{1,0:T(8,128)} %get-tuple-element.118.refs_, ...), custom_call_target="tpu_custom_call" | custom-call | tf_op jit(solution)/shard_map/pallas_call | solution.py:666
  216.2 4.9 %convolution_add_fusion = f32[256,1024]{1,0:T(8,128)} fusion(f32[256,1024]{1,0:T(8,128)S(1)} %copy-done.3, bf16[256,2048]{1,0:T(8,128)(2,1)} %get-tuple-element.67, bf16[2048,1024]{1,0:T(8,128)(2,1)} %bitcast.88), kind=kOutput, calls=%fused_computation.6 | convolution fusion | flops 1074003968 | bytes 7340032 | tf_op jit(solution)/shard_map/dot_general | solution.py:29
  221.1 2.7 convolution_bitcast_fusion.refs_0_
  223.8 3.3 convolution_convert_fusion.3
  227.0 70.2 %shard_map.223 = (bf16[256,4096]{1,0:T(8,128)(2,1)}, bf16[192,2048]{1,0:T(8,128)(2,1)}, f32[64,1024]{1,0:T(8,128)}) custom-call(f32[256,2048]{1,0:T(8,128)} %convolution_bitcast_fusion.refs_0_, f32[256,2048]{1,0:T(8,128)} %get-tuple-element.69.refs_1_, bf16[256,2048]{1,0:T(8,128)(2,1)} %get-tuple-element.70.refs_2_, ...), custom_call_target="tpu_custom_call" | custom-call | tf_op jit(solution)/shard_map/pallas_call | solution.py:666
  297.3 7.2 %multiply_reduce_fusion = (f32[1024]{0:T(1024)}, f32[256]{0:T(256)S(1)}, f32[256,1024]{1,0:T(8,128)S(1)}) fusion(f32[256,1024]{1,0:T(8,128)S(1)} %copy-done.3, f32[256]{0:T(256)S(1)} %add_rsqrt_fusion, f32[1024]{0:T(1024)S(1)} %bitcast.85, bf16[256,4096]{1,0:T(8,128)(2,1)} %get-tuple-element.80, bf16[4096,1024]{1,0:T(8,128)(2,1)} %bitcast.63), kind=kOutput, calls=%fused_computation.9 | convolution fusion | flops 2149055232 | bytes 12593152 | tf_op jit(solution)/shard_map/dot_general | solution.py:29
  304.9 2.7 fusion.1.refs_0_
  307.6 3.3 convolution_convert_fusion.2
  310.9 5.6 %convolution_convert_fusion.1 = bf16[4096,1024]{1,0:T(8,128)(2,1)} fusion(bf16[256,4096]{1,0:T(8,128)(2,1)S(1)} %copy-done.5, bf16[256,1024]{1,0:T(8,128)(2,1)S(1)} %copy-done.12), kind=kOutput, calls=%fused_computation.1 | convolution fusion | flops 2151677952 | bytes 11010048 | tf_op jit(solution)/shard_map/dot_general | solution.py:1633
  316.5 79.1 %shard_map.224 = (bf16[256,4096]{1,0:T(8,128)(2,1)}, bf16[192,2048]{1,0:T(8,128)(2,1)}, f32[128,1024]{1,0:T(8,128)}, f32[64,1024]{1,0:T(8,128)}) custom-call(f32[256,2048]{1,0:T(8,128)} %fusion.1.refs_0_, f32[256,2048]{1,0:T(8,128)} %get-tuple-element.81.refs_1_, bf16[256,2048]{1,0:T(8,128)(2,1)} %get-tuple-element.82.refs_2_, ...), custom_call_target="tpu_custom_call" | custom-call | tf_op jit(solution)/shard_map/pallas_call | solution.py:666
  395.6 1.3 pad_maximum_fusion
  397.5 1.5 copy.28
  399.0 0.8 pad_maximum_fusion.2
  399.8 5.6 %convolution_convert_fusion = bf16[4096,1024]{1,0:T(8,128)(2,1)} fusion(bf16[256,4096]{1,0:T(8,128)(2,1)S(1)} %copy-done.1, bf16[256,1024]{1,0:T(8,128)(2,1)S(1)} %copy-done.11), kind=kOutput, calls=%fused_computation | convolution fusion | flops 2151677952 | bytes 11010048 | tf_op jit(solution)/shard_map/dot_general | solution.py:1633
  405.4 61.4 %shard_map.225 = (f32[256,1024]{1,0:T(8,128)}, f32[128,1024]{1,0:T(8,128)}, f32[2,1024]{1,0:T(2,128)}, f32[2,96,256]{2,1,0:T(8,128)}, f32[2,64,256]{2,1,0:T(8,12...) custom-call(bf16[2,2,4,2,96,256]{5,4,3,2,1,0:T(8,128)(2,1)} %bitcast, ...), custom_call_target="tpu_custom_call" | custom-call | tf_op jit(solution)/shard_map/pallas_call | solution.py:1419
  467.0 2.2 pad_maximum_fusion.1
  469.2 2.3 copy.40
  471.5 0.6 copy.41
  472.1 0.6 copy.42
  472.7 0.6 copy.43
  473.3 0.7 copy.44
  474.0 0.7 copy.45
  475.2 0.6 copy.47
  475.8 0.6 copy.48
  (64 shorter events, 1.8 us)
Async XLA Ops:
  78.5 71.5 %copy-start.2 = (bf16[2,2,4,2,64,1024]{5,4,3,2,1,0:T(8,128)(2,1)S(1)}, bf16[2,2,4,2,64,1024]{5,4,3,2,1,0:T(8,128)(2,1)}, u32[]{:S(2)}) copy-start(bf16[2,2,4,2,64,1024]{5,4,3,2,1,0:T(8,128)(2,1)} %get-tuple-element.65) | copy-start | bytes 12582916
  78.5 71.5 %copy-start.8 = (bf16[2,128,1024]{2,1,0:T(8,128)(2,1)S(1)}, bf16[2,128,1024]{2,1,0:T(8,128)(2,1)}, u32[]{:S(2)}) copy-start(bf16[2,128,1024]{2,1,0:T(8,128)(2,1)} %param.13) | copy-start | bytes 1572868
  153.4 62.8 %copy-start.3 = (f32[256,1024]{1,0:T(8,128)S(1)}, f32[256,1024]{1,0:T(8,128)}, u32[]{:S(2)}) copy-start(f32[256,1024]{1,0:T(8,128)} %get-tuple-element.118.refs_0_) | copy-start | bytes 3145732
  216.1 4.9 %copy-start.9 = (bf16[2,128,1024]{2,1,0:T(8,128)(2,1)S(1)}, bf16[2,128,1024]{2,1,0:T(8,128)(2,1)}, u32[]{:S(2)}) copy-start(bf16[2,128,1024]{2,1,0:T(8,128)(2,1)} %param.25) | copy-start | bytes 1572868
  216.2 4.9 %copy-start.25 = (bf16[2,2,4,2,64,1024]{5,4,3,2,1,0:T(8,128)(2,1)S(1)}, bf16[2,2,4,2,64,1024]{5,4,3,2,1,0:T(8,128)(2,1)}, u32[]{:S(2)}) copy-start(bf16[2,2,4,2,64,1024]{5,4,3,2,1,0:T(8,128)(2,1)} %get-tuple-element.68) | copy-start | bytes 12582916
  221.1 2.7 copy-start.7
  227.0 70.3 %copy-start.18 = (f32[1,1024]{1,0:T(1,128)S(1)}, f32[1,1024]{1,0:T(1,128)}, u32[]{:S(2)}) copy-start(f32[1,1024]{1,0:T(1,128)} %get-tuple-element.112.refs_1_) | copy-start | bytes 12292
  297.3 7.2 %copy-start.4 = (f32[256,1024]{1,0:T(8,128)S(1)}, f32[256,1024]{1,0:T(8,128)}, u32[]{:S(2)}) copy-start(f32[256,1024]{1,0:T(8,128)} %get-tuple-element.118.refs_0_) | copy-start | bytes 3145732
  304.9 6.0 %copy-start = (f32[256,1024]{1,0:T(8,128)}, f32[256,1024]{1,0:T(8,128)S(1)}, u32[]{:S(2)}) copy-start(f32[256,1024]{1,0:T(8,128)S(1)} %multiply_add_fusion.flow_ref) | copy-start | bytes 3145732
  304.9 2.7 copy-start.6
  307.6 3.3 copy-start.5
  307.6 3.3 copy-start.12
  316.5 79.1 %copy-start.10 = (bf16[192,2048]{1,0:T(8,128)(2,1)S(1)}, bf16[192,2048]{1,0:T(8,128)(2,1)}, u32[]{:S(2)}) copy-start(bf16[192,2048]{1,0:T(8,128)(2,1)} %get-tuple-element.94) | copy-start | bytes 2359300
  395.6 3.4 copy-start.14
  395.6 3.4 copy-start.15
  396.9 2.9 copy-start.1
  396.9 2.9 copy-start.11
  405.4 61.5 %copy-start.13 = (f32[128,1024]{1,0:T(8,128)S(1)}, f32[128,1024]{1,0:T(8,128)}, u32[]{:S(2)}) copy-start(f32[128,1024]{1,0:T(8,128)} %get-tuple-element.100) | copy-start | bytes 1572868
  466.9 4.6 copy-start.21
  466.9 5.2 %copy-start.20 = (f32[2,4,256]{2,1,0:T(4,128)S(1)}, f32[2,4,256]{2,1,0:T(4,128)}, u32[]{:S(2)}) copy-start(f32[2,4,256]{2,1,0:T(4,128)} %get-tuple-element.141) | copy-start | bytes 24580
  466.9 5.8 %copy-start.24 = (f32[2,256]{1,0:T(2,128)S(1)}, f32[2,256]{1,0:T(2,128)}, u32[]{:S(2)}) copy-start(f32[2,256]{1,0:T(2,128)} %get-tuple-element.142) | copy-start | bytes 6148
  466.9 6.4 %copy-start.16 = (f32[2,96,256]{2,1,0:T(8,128)S(1)}, f32[2,96,256]{2,1,0:T(8,128)}, u32[]{:S(2)}) copy-start(f32[2,96,256]{2,1,0:T(8,128)} %get-tuple-element.105) | copy-start | bytes 589828
  466.9 7.0 %copy-start.17 = (f32[2,64,256]{2,1,0:T(8,128)S(1)}, f32[2,64,256]{2,1,0:T(8,128)}, u32[]{:S(2)}) copy-start(f32[2,64,256]{2,1,0:T(8,128)} %get-tuple-element.144) | copy-start | bytes 393220
  466.9 7.7 %copy-start.23 = (f32[2,256]{1,0:T(2,128)S(1)}, f32[2,256]{1,0:T(2,128)}, u32[]{:S(2)}) copy-start(f32[2,256]{1,0:T(2,128)} %get-tuple-element.145) | copy-start | bytes 6148
  466.9 8.3 %copy-start.19 = (f32[2,16,256]{2,1,0:T(8,128)S(1)}, f32[2,16,256]{2,1,0:T(8,128)}, u32[]{:S(2)}) copy-start(f32[2,16,256]{2,1,0:T(8,128)} %get-tuple-element.146) | copy-start | bytes 98308
  467.0 8.9 %copy-start.22 = (f32[2,256]{1,0:T(2,128)S(1)}, f32[2,256]{1,0:T(2,128)}, u32[]{:S(2)}) copy-start(f32[2,256]{1,0:T(2,128)} %get-tuple-element.147) | copy-start | bytes 6148

commit v3 on v2

--- a/solution.py
+++ b/solution.py
@@ -255,7 +255,7 @@
     dsts, refs = refs[:n], refs[n:]
     (proj_s, x_s, tail_s, halo_s, act_s, z_s, rank2_s, cd_s, eff_s, u_s, sa, sb, y_s, delta_s, end_s, start_s,
      sum_s), refs = refs[:17], refs[17:]
-    exch, (send, recv, hsend, hrecv) = refs[:10], refs[10:]
+    exch, (send, recv, hsend, hrecv) = refs[:20], refs[20:]
     here = Place()
     block = pl.program_id(0)
     front = 2 * narrow
@@ -274,6 +274,7 @@
             h * lax.rsqrt(jnp.mean(h * h, axis=1, keepdims=True) + norm_eps) * gain_ref[...]
         ).astype(bf16)
 
+    exchanges(here, False, rows, end_s, sum_s, rates_ref, start_s, exch, block, front + blocks // 2)
     jobs = [
         Gather(here, src.at[layer], dst, send, recv, GATHER_SEMS * i)
         for i, (src, dst, layer) in enumerate(zip(srcs, dsts, layer_of))
@@ -327,7 +328,6 @@
     @pl.when(block == front + blocks - 1)
     def _():
         sum_ref[...] = sum_s[...]
-        exchange(here, False, rows, end_s, sum_s, rates_ref, start_s, exch)
 
     @pl.when(block >= front + blocks)
     def _():
@@ -492,7 +492,7 @@
     (weff_s, wgy_s, gyall_s, end_s, start_s, gz_s, gact_s, gproj_s, gproj_t_s, gend_s, edge_s, late_s, gdtw_s, gbias_s, grate_s,
      gskip_s, gxp_s, gkern_s, goff_s), refs = refs[:19], refs[19:]
     (eff_s, u_s, gy_s, fade_s, held_s, sa, sb, gu_s, gd_s, gb_s, gc_s, grank_s), refs = refs[:12], refs[12:]
-    exch, (esend, erecv), refs = refs[:10], refs[10:12], refs[12:]
+    exch, (esend, erecv), refs = refs[:20], refs[20:22], refs[22:]
     here = Place()
     block = pl.program_id(0)
     wide_cb, cb = gg_ref.shape[1], act_ref.shape[1]
@@ -508,6 +508,7 @@
         gb_s[...] = jnp.zeros_like(gb_s)
         grank_s[...] = jnp.zeros_like(grank_s)
 
+    exchanges(here, True, rows, end_s, sum_ref, rates_ref, start_s, exch, block, blocks // 2)
     beside(Reduces(srcs, sums, refs), block, BACKWARD_STEPS)
 
     @pl.when(block < blocks)
@@ -519,10 +520,6 @@
         mixed_ref[:, pl.ds(pl.multiple_of(c + block * wide_cb, wide_cb), wide_cb)] = gz_s[...]
         gyall_s[:, cols] = gy.astype(f32)
         end_s[:, cols] = flow
-
-    @pl.when(block == blocks - 1)
-    def _():
-        exchange(here, True, rows, end_s, sum_ref, rates_ref, start_s, exch)
 
     @pl.when((block >= blocks) & (block < blocks + narrow))
     def _():
@@ -752,7 +749,7 @@
              pltpu.VMEM((t, 2 * self.rank), bf16), pltpu.VMEM((t // STEPS, STEPS, self.inner), f32),
              self.scratch3(cb), self.scratch3(cb), self.wide_scratch(bf16, cb), self.wide_scratch(bf16, cb),
              self.scratch3(cb), pltpu.VMEM((blocks, t, cb), f32), pltpu.VMEM((sn, c), f32), pltpu.VMEM((sn, c), f32),
-             pltpu.VMEM((self.rows, c), f32)] + exchange_scratch(self.rows, sn, c) + sems,
+             pltpu.VMEM((self.rows, c), f32)] + exchange_scratch(self.rows, sn, c // 2) * 2 + sems,
             (h, gain, in_full, in_full, full, half, masks, half, kill, full, full, *[g for g, _ in gathers]),
             ident,
         )
@@ -799,7 +796,7 @@
             + [pltpu.VMEM((narrow, k, cb), f32) for k in (self.rank, 1, ns, 1)]
             + [pltpu.VMEM((k, cb), f32) for k in (self.width, self.taps, 1)]
             + [self.scratch3(cb)] * 3 + [self.wide_scratch(f32, cb)] * 4 + [self.scratch3(cb)] * 2
-            + [pltpu.VMEM(tall, f32)] * 2 + [pltpu.VMEM((t, self.rank), f32)] + exchange_scratch(self.rows, sn, c)
+            + [pltpu.VMEM(tall, f32)] * 2 + [pltpu.VMEM((t, self.rank), f32)] + exchange_scratch(self.rows, sn, c // 2) * 2
             + sems + more_scratch,
             (gg, z, y, delta, full, kill, full, total, act, delta, full, half, m["rank_t"], m["bb"], m["cc"], keep, x, halo,
              masks, *more_in),
@@ -1438,56 +1435,92 @@
     ]
 
 
-def exchange(here, backward, rows, end_ref, sum_ref, rate_ref, out_ref, scratch):
-    sent, back, got, late, gsum, msum, line, lsum, send, recv = scratch
-    half = end_ref.shape[1] // 2
-    mine = pl.ds(pl.multiple_of(here.c * half, half), half)
-    theirs = pl.ds(pl.multiple_of((1 - here.c) * half, half), half)
-    other = here.at(c=1 - here.c)
-    sent[...] = end_ref[:, theirs].astype(bf16)
-    msum[0] = sum_ref[:, theirs]
-    one = [push(sent, got, send, recv, 0, other), push(msum.at[0], gsum, send, recv, 1, other)]
-    for copy in one:
-        copy.start()
-    rate = rate_ref[:, mine]
-
-    def fade(total):
-        return jnp.concatenate([jnp.exp(rate * total[s : s + 1]) for s in range(rows)], axis=0)
-
-    for copy in one:
-        copy.wait()
-    e_me, d_me = end_ref[:, mine], sum_ref[:, mine]
-    e_it, d_it = got[...].astype(f32), gsum[...]
-    first = here.c == 0
-    e0, e1 = jnp.where(first, e_me, e_it), jnp.where(first, e_it, e_me)
-    d0, d1 = jnp.where(first, d_me, d_it), jnp.where(first, d_it, d_me)
-    chip = e0 + fade(d0) * e1 if backward else fade(d1) * e0 + e1
-    line[3] = chip.astype(bf16)
-    lsum[3] = d0 + d1
-    two = []
-    for k in (1, 2, 3):
-        two.append(push(line.at[3], line.at[k - 1], send, recv, 2 + 2 * k, here.at(z=here.over(k))))
-        two.append(push(lsum.at[3], lsum.at[k - 1], send, recv, 3 + 2 * k, here.at(z=here.over(k))))
-    for copy in two:
-        copy.start()
-    for copy in two:
-        copy.wait()
-    state = jnp.zeros_like(chip)
-    for k in (1, 2, 3) if backward else (3, 2, 1):
-        at = lax.rem(here.z + 4 - k, 4)
-        e, d = line[k - 1].astype(f32), lsum[k - 1]
-        use = at > here.z if backward else at < here.z
-        state = jnp.where(use, fade(d) * state + e, state)
-    if backward:
-        s1, s0 = state, e1 + fade(d1) * state
-    else:
-        s0, s1 = state, fade(d0) * state + e0
-    out_ref[:, mine] = jnp.where(first, s0, s1)
-    back[...] = jnp.where(first, s1, s0).astype(bf16)
-    three = push(back, late, send, recv, 2, other)
-    three.start()
-    three.wait()
-    out_ref[:, theirs] = late[...].astype(f32)
+class Exchange:
+    def __init__(self, here, backward, rows, end_ref, sum_ref, rate_ref, out_ref, scratch, off, width):
+        self.here, self.backward, self.rows = here, backward, rows
+        self.end, self.sum, self.out = end_ref, sum_ref, out_ref
+        self.sent, self.back, self.got, self.late, self.gsum, self.msum, self.line, self.lsum, self.send, self.recv = scratch
+        half = width // 2
+        self.mine = pl.ds(pl.multiple_of(off + here.c * half, half), half)
+        self.theirs = pl.ds(pl.multiple_of(off + (1 - here.c) * half, half), half)
+        self.other = here.at(c=1 - here.c)
+        self.rate = rate_ref
+        self.phases = [self.begin, self.second, self.third, self.last]
+
+    def one(self):
+        return [push(self.sent, self.got, self.send, self.recv, 0, self.other),
+                push(self.msum.at[0], self.gsum, self.send, self.recv, 1, self.other)]
+
+    def two(self):
+        out = []
+        for k in (1, 2, 3):
+            to = self.here.at(z=self.here.over(k))
+            out.append(push(self.line.at[3], self.line.at[k - 1], self.send, self.recv, 2 + 2 * k, to))
+            out.append(push(self.lsum.at[3], self.lsum.at[k - 1], self.send, self.recv, 3 + 2 * k, to))
+        return out
+
+    def three(self):
+        return push(self.back, self.late, self.send, self.recv, 2, self.other)
+
+    def fade(self, total):
+        rate = self.rate[:, self.mine]
+        return jnp.concatenate([jnp.exp(rate * total[s : s + 1]) for s in range(self.rows)], axis=0)
+
+    def pair(self):
+        e_me, d_me = self.end[:, self.mine], self.sum[:, self.mine]
+        e_it, d_it = self.got[...].astype(f32), self.gsum[...]
+        first = self.here.c == 0
+        return (jnp.where(first, e_me, e_it), jnp.where(first, e_it, e_me),
+                jnp.where(first, d_me, d_it), jnp.where(first, d_it, d_me))
+
+    def begin(self):
+        self.sent[...] = self.end[:, self.theirs].astype(bf16)
+        self.msum[0] = self.sum[:, self.theirs]
+        for copy in self.one():
+            copy.start()
+
+    def second(self):
+        for copy in self.one():
+            copy.wait()
+        e0, e1, d0, d1 = self.pair()
+        chip = e0 + self.fade(d0) * e1 if self.backward else self.fade(d1) * e0 + e1
+        self.line[3] = chip.astype(bf16)
+        self.lsum[3] = d0 + d1
+        for copy in self.two():
+            copy.start()
+
+    def third(self):
+        for copy in self.two():
+            copy.wait()
+        e0, e1, d0, d1 = self.pair()
+        state = jnp.zeros_like(e0)
+        z = self.here.z
+        for k in (1, 2, 3) if self.backward else (3, 2, 1):
+            at = lax.rem(z + 4 - k, 4)
+            e, d = self.line[k - 1].astype(f32), self.lsum[k - 1]
+            use = at > z if self.backward else at < z
+            state = jnp.where(use, self.fade(d) * state + e, state)
+        if self.backward:
+            s1, s0 = state, e1 + self.fade(d1) * state
+        else:
+            s0, s1 = state, self.fade(d0) * state + e0
+        first = self.here.c == 0
+        self.out[:, self.mine] = jnp.where(first, s0, s1)
+        self.back[...] = jnp.where(first, s1, s0).astype(bf16)
+        self.three().start()
+
+    def last(self):
+        self.three().wait()
+        self.out[:, self.theirs] = self.late[...].astype(f32)
+
+
+def exchanges(here, backward, rows, end_ref, sum_ref, rate_ref, out_ref, scratch, block, first):
+    width = end_ref.shape[1] // 2
+    for i in range(2):
+        work = Exchange(here, backward, rows, end_ref, sum_ref, rate_ref, out_ref, scratch[10 * i : 10 * i + 10],
+                        i * width, width)
+        at = first + 2 * i
+        beside(work, block, (at, at + 1, at + 2, at + 2))
 
 
 def carried_in(ends, sums, rate, axis, backward):

time: 486 us -> 478 us (0.984)
  Pallas kernels: 418 us -> 409 us
    pallas_call x4, Pallas kernels: 283 us -> 275 us  [call(): pl.pallas_call(body, grid=(blocks,), in_specs=ins, out_specs=[spec for sp...]
where the time goes in v3:
time: 478 us; the launch traced here: 468 us
  Pallas kernels  409 us (86%)
  matrix products  38.7 us (8%)
  local copies, waits for them, and re-layouts  11.7 us (2%)
  other arithmetic  7.05 us (1%)
    pallas_call x4, Pallas kernels, call(): pl.pallas_call(body, grid=(blocks,), in_specs=ins, out_specs=[spec for sp...  275 us
    pallas_call x1, Pallas kernels, gather_all(): pl.pallas_call(gather_kernel, out_shape=outs, in_specs=[INV] * 7 + [ANY]...  73 us
    pallas_call x1, Pallas kernels, finish(): pl.pallas_call(functools.partial(finish_kernel, cuts), out_shape=outs, in...  61.6 us
    dot_general x3, matrix products, dot(): return jnp.dot(a, b, preferred_element_type=f32)  15.6 us
    dot_general x2, matrix products, body(): lax.dot_general(mixed, normed, (((0,), (0,)), ((), ())), preferred_elemen...  11.2 us

profile of v3, /device:TPU:0, one launch (start us, length us, event | category | flops | bytes accessed | tf_op | source)
XLA Modules:
  0.0 468.4 jit_solution(12715560779776138488)
XLA Ops:
  0.7 0.8 compare_reduce_fusion
  1.4 0.8 select_reduce_fusion
  2.2 1.4 fusion.6
  3.6 0.8 broadcast_in_dim.23.refs_8_.refs_5_
  4.7 0.8 pad_maximum_fusion.3.refs_6_.refs_18_
  5.4 73.0 %shard_map.220 = (bf16[320,2048]{1,0:T(8,128)(2,1)}, f32[64,2048]{1,0:T(8,128)}, bf16[2,2,4,2,128,1024]{5,4,3,2,1,0:T(8,128)(2,1)}, bf16[2,2,4,2,64,1024]{5,4,3,2,1,0:T(8,128)(2,1)}) custom-call(bf16[2,96,256]{2,1,0:T(8,128)(2,1)} %bitcast.84, bf16[2,64,256]{2,1,0:T(8,128)(2,1)} %dtw_ref.1, f32[2,16,256]{2,1,0:T(8,128)} %rate_ref.1, f32[2,4,256]{2,1,0:T(4,128)} %kern_ref.1, ...), custom_call_target="tpu_custom_call" | custom-call | tf_op jit(solution)/shard_map/pallas_call | solution.py:1127
  78.5 69.1 %shard_map.221 = (bf16[256,1024]{1,0:T(8,128)(2,1)}, bf16[256,2048]{1,0:T(8,128)(2,1)}, f32[256,2048]{1,0:T(8,128)}, bf16[16,2048]{1,0:T(8,128)(2,1)}, f32[256,2...) custom-call(bf16[256,1024]{1,0:T(8,128)(2,1)} %bitcast.71, ...), custom_call_target="tpu_custom_call" | custom-call | tf_op jit(solution)/shard_map/pallas_call | solution.py:663
  147.7 3.5 multiply_reduce_fusion.2
  151.1 58.3 %shard_map.222 = (bf16[256,1024]{1,0:T(8,128)(2,1)}, bf16[256,2048]{1,0:T(8,128)(2,1)}, f32[256,2048]{1,0:T(8,128)}, bf16[16,2048]{1,0:T(8,128)(2,1)}, f32[256,2...) custom-call(f32[256,1024]{1,0:T(8,128)} %get-tuple-element.118.refs_, ...), custom_call_target="tpu_custom_call" | custom-call | tf_op jit(solution)/shard_map/pallas_call | solution.py:663
  209.5 4.9 %convolution_add_fusion = f32[256,1024]{1,0:T(8,128)} fusion(f32[256,1024]{1,0:T(8,128)S(1)} %copy-done.3, bf16[256,2048]{1,0:T(8,128)(2,1)} %get-tuple-element.67, bf16[2048,1024]{1,0:T(8,128)(2,1)} %bitcast.88), kind=kOutput, calls=%fused_computation.6 | convolution fusion | flops 1074003968 | bytes 7340032 | tf_op jit(solution)/shard_map/dot_general | solution.py:29
  214.4 2.7 convolution_bitcast_fusion.refs_0_
  217.1 3.3 convolution_convert_fusion.3
  220.3 65.4 %shard_map.223 = (bf16[256,4096]{1,0:T(8,128)(2,1)}, bf16[192,2048]{1,0:T(8,128)(2,1)}, f32[64,1024]{1,0:T(8,128)}) custom-call(f32[256,2048]{1,0:T(8,128)} %convolution_bitcast_fusion.refs_0_, f32[256,2048]{1,0:T(8,128)} %get-tuple-element.69.refs_1_, bf16[256,2048]{1,0:T(8,128)(2,1)} %get-tuple-element.70.refs_2_, ...), custom_call_target="tpu_custom_call" | custom-call | tf_op jit(solution)/shard_map/pallas_call | solution.py:663
  285.7 7.2 %multiply_reduce_fusion = (f32[1024]{0:T(1024)}, f32[256]{0:T(256)S(1)}, f32[256,1024]{1,0:T(8,128)S(1)}) fusion(f32[256,1024]{1,0:T(8,128)S(1)} %copy-done.3, f32[256]{0:T(256)S(1)} %add_rsqrt_fusion, f32[1024]{0:T(1024)S(1)} %bitcast.85, bf16[256,4096]{1,0:T(8,128)(2,1)} %get-tuple-element.80, bf16[4096,1024]{1,0:T(8,128)(2,1)} %bitcast.63), kind=kOutput, calls=%fused_computation.9 | convolution fusion | flops 2149055232 | bytes 12593152 | tf_op jit(solution)/shard_map/dot_general | solution.py:29
  293.3 2.7 fusion.1.refs_0_
  296.0 3.3 convolution_convert_fusion.2
  299.3 5.6 %convolution_convert_fusion.1 = bf16[4096,1024]{1,0:T(8,128)(2,1)} fusion(bf16[256,4096]{1,0:T(8,128)(2,1)S(1)} %copy-done.5, bf16[256,1024]{1,0:T(8,128)(2,1)S(1)} %copy-done.12), kind=kOutput, calls=%fused_computation.1 | convolution fusion | flops 2151677952 | bytes 11010048 | tf_op jit(solution)/shard_map/dot_general | solution.py:1666
  304.9 82.1 %shard_map.224 = (bf16[256,4096]{1,0:T(8,128)(2,1)}, bf16[192,2048]{1,0:T(8,128)(2,1)}, f32[128,1024]{1,0:T(8,128)}, f32[64,1024]{1,0:T(8,128)}) custom-call(f32[256,2048]{1,0:T(8,128)} %fusion.1.refs_0_, f32[256,2048]{1,0:T(8,128)} %get-tuple-element.81.refs_1_, bf16[256,2048]{1,0:T(8,128)(2,1)} %get-tuple-element.82.refs_2_, ...), custom_call_target="tpu_custom_call" | custom-call | tf_op jit(solution)/shard_map/pallas_call | solution.py:663
  387.0 1.3 pad_maximum_fusion
  388.9 1.5 copy.28
  390.4 0.8 pad_maximum_fusion.2
  391.2 5.6 %convolution_convert_fusion = bf16[4096,1024]{1,0:T(8,128)(2,1)} fusion(bf16[256,4096]{1,0:T(8,128)(2,1)S(1)} %copy-done.1, bf16[256,1024]{1,0:T(8,128)(2,1)S(1)} %copy-done.11), kind=kOutput, calls=%fused_computation | convolution fusion | flops 2151677952 | bytes 11010048 | tf_op jit(solution)/shard_map/dot_general | solution.py:1666
  396.8 61.6 %shard_map.225 = (f32[256,1024]{1,0:T(8,128)}, f32[128,1024]{1,0:T(8,128)}, f32[2,1024]{1,0:T(2,128)}, f32[2,96,256]{2,1,0:T(8,128)}, f32[2,64,256]{2,1,0:T(8,12...) custom-call(bf16[2,2,4,2,96,256]{5,4,3,2,1,0:T(8,128)(2,1)} %bitcast, ...), custom_call_target="tpu_custom_call" | custom-call | tf_op jit(solution)/shard_map/pallas_call | solution.py:1416
  458.5 2.2 pad_maximum_fusion.1
  460.7 2.3 copy.40
  463.0 0.6 copy.41
  463.6 0.6 copy.42
  464.2 0.6 copy.43
  464.8 0.7 copy.44
  465.5 0.7 copy.45
  466.1 0.6 copy.46
  466.7 0.6 copy.47
  (64 shorter events, 1.8 us)
Async XLA Ops:
  78.5 69.2 %copy-start.2 = (bf16[2,2,4,2,64,1024]{5,4,3,2,1,0:T(8,128)(2,1)S(1)}, bf16[2,2,4,2,64,1024]{5,4,3,2,1,0:T(8,128)(2,1)}, u32[]{:S(2)}) copy-start(bf16[2,2,4,2,64,1024]{5,4,3,2,1,0:T(8,128)(2,1)} %get-tuple-element.65) | copy-start | bytes 12582916
  78.5 69.2 %copy-start.8 = (bf16[2,128,1024]{2,1,0:T(8,128)(2,1)S(1)}, bf16[2,128,1024]{2,1,0:T(8,128)(2,1)}, u32[]{:S(2)}) copy-start(bf16[2,128,1024]{2,1,0:T(8,128)(2,1)} %param.13) | copy-start | bytes 1572868
  151.1 58.3 %copy-start.3 = (f32[256,1024]{1,0:T(8,128)S(1)}, f32[256,1024]{1,0:T(8,128)}, u32[]{:S(2)}) copy-start(f32[256,1024]{1,0:T(8,128)} %get-tuple-element.118.refs_0_) | copy-start | bytes 3145732
  209.4 4.9 %copy-start.9 = (bf16[2,128,1024]{2,1,0:T(8,128)(2,1)S(1)}, bf16[2,128,1024]{2,1,0:T(8,128)(2,1)}, u32[]{:S(2)}) copy-start(bf16[2,128,1024]{2,1,0:T(8,128)(2,1)} %param.25) | copy-start | bytes 1572868
  209.5 4.9 %copy-start.25 = (bf16[2,2,4,2,64,1024]{5,4,3,2,1,0:T(8,128)(2,1)S(1)}, bf16[2,2,4,2,64,1024]{5,4,3,2,1,0:T(8,128)(2,1)}, u32[]{:S(2)}) copy-start(bf16[2,2,4,2,64,1024]{5,4,3,2,1,0:T(8,128)(2,1)} %get-tuple-element.68) | copy-start | bytes 12582916
  214.4 2.7 copy-start.7
  220.3 65.4 %copy-start.18 = (f32[1,1024]{1,0:T(1,128)S(1)}, f32[1,1024]{1,0:T(1,128)}, u32[]{:S(2)}) copy-start(f32[1,1024]{1,0:T(1,128)} %get-tuple-element.112.refs_1_) | copy-start | bytes 12292
  285.7 7.2 %copy-start.4 = (f32[256,1024]{1,0:T(8,128)S(1)}, f32[256,1024]{1,0:T(8,128)}, u32[]{:S(2)}) copy-start(f32[256,1024]{1,0:T(8,128)} %get-tuple-element.118.refs_0_) | copy-start | bytes 3145732
  293.3 6.0 %copy-start = (f32[256,1024]{1,0:T(8,128)}, f32[256,1024]{1,0:T(8,128)S(1)}, u32[]{:S(2)}) copy-start(f32[256,1024]{1,0:T(8,128)S(1)} %multiply_add_fusion.flow_ref) | copy-start | bytes 3145732
  293.3 2.7 copy-start.6
  295.9 3.3 copy-start.5
  296.0 3.3 copy-start.12
  304.9 82.1 %copy-start.10 = (bf16[192,2048]{1,0:T(8,128)(2,1)S(1)}, bf16[192,2048]{1,0:T(8,128)(2,1)}, u32[]{:S(2)}) copy-start(bf16[192,2048]{1,0:T(8,128)(2,1)} %get-tuple-element.94) | copy-start | bytes 2359300
  387.0 3.4 copy-start.14
  387.0 3.4 copy-start.15
  388.3 2.9 copy-start.1
  388.3 2.9 copy-start.11
  396.8 61.7 %copy-start.13 = (f32[128,1024]{1,0:T(8,128)S(1)}, f32[128,1024]{1,0:T(8,128)}, u32[]{:S(2)}) copy-start(f32[128,1024]{1,0:T(8,128)} %get-tuple-element.100) | copy-start | bytes 1572868
  458.4 4.6 copy-start.21
  458.4 5.2 %copy-start.20 = (f32[2,4,256]{2,1,0:T(4,128)S(1)}, f32[2,4,256]{2,1,0:T(4,128)}, u32[]{:S(2)}) copy-start(f32[2,4,256]{2,1,0:T(4,128)} %get-tuple-element.141) | copy-start | bytes 24580
  458.4 5.8 %copy-start.24 = (f32[2,256]{1,0:T(2,128)S(1)}, f32[2,256]{1,0:T(2,128)}, u32[]{:S(2)}) copy-start(f32[2,256]{1,0:T(2,128)} %get-tuple-element.142) | copy-start | bytes 6148
  458.4 6.4 %copy-start.16 = (f32[2,96,256]{2,1,0:T(8,128)S(1)}, f32[2,96,256]{2,1,0:T(8,128)}, u32[]{:S(2)}) copy-start(f32[2,96,256]{2,1,0:T(8,128)} %get-tuple-element.105) | copy-start | bytes 589828
  458.4 7.0 %copy-start.17 = (f32[2,64,256]{2,1,0:T(8,128)S(1)}, f32[2,64,256]{2,1,0:T(8,128)}, u32[]{:S(2)}) copy-start(f32[2,64,256]{2,1,0:T(8,128)} %get-tuple-element.144) | copy-start | bytes 393220
  458.5 7.7 %copy-start.23 = (f32[2,256]{1,0:T(2,128)S(1)}, f32[2,256]{1,0:T(2,128)}, u32[]{:S(2)}) copy-start(f32[2,256]{1,0:T(2,128)} %get-tuple-element.145) | copy-start | bytes 6148
  458.5 8.3 %copy-start.19 = (f32[2,16,256]{2,1,0:T(8,128)S(1)}, f32[2,16,256]{2,1,0:T(8,128)}, u32[]{:S(2)}) copy-start(f32[2,16,256]{2,1,0:T(8,128)} %get-tuple-element.146) | copy-start | bytes 98308
  458.5 8.9 %copy-start.22 = (f32[2,256]{1,0:T(2,128)S(1)}, f32[2,256]{1,0:T(2,128)}, u32[]{:S(2)}) copy-start(f32[2,256]{1,0:T(2,128)} %get-tuple-element.147) | copy-start | bytes 6148
